TPU v7x, 256 devices: a whole 4x4x8 slice. The times are simulated.
256 devices in a mesh: group: 16 (over z, core), dev: 16 (over y, x).
Axes of the slice: x: 4, y: 4, z: 8, core: 2. Of those that a mesh axis runs over, the one named last changes fastest.
Arguments:
- applied_loads: float32 [256, 1536, 128], P(('group', 'dev'))
- stiffness: bfloat16 [256, 1536, 1536], P(('group', 'dev')), as said below
- local_inverse: bfloat16 [256, 1536, 1536], P(('group', 'dev')), as said below
- coarse_basis: bfloat16 [256, 48, 1536], P(('group', 'dev')), may hold values from -0.15625 to 0.15625
- face_index: int32 [256, 1536], P(('group', 'dev')), may hold values from 0 to 1535, each once within a row
- coarse_map: int32 [256, 48], P(('group', 'dev')), may hold values from 0 to 47, each once within a row
- group_inverse: float32 [12288, 768], P(('group', 'dev')), as said below
- top_basis: float32 [12288, 48], P(('group', 'dev')), may hold values from -0.875 to 0.875
- top_inverse: float32 [768, 768], P('group'), as said below
Outputs:
- solution: float32 [256, 1536, 128], P(('group', 'dev'))
- residual: float32 [256, 1536, 128], P(('group', 'dev'))
- direction: float32 [256, 1536, 128], P(('group', 'dev'))
Inputs may be any that keep to these rules, and one draw needn't show every extreme that they name: `stiffness`: each subdomain's block is symmetric positive definite. `local_inverse`: each subdomain's block is symmetric positive definite. `group_inverse`: each group's block of 768 rows is symmetric positive definite. `top_inverse`: symmetric positive definite. `face_index`: each row is a permutation. `coarse_map`: each row is a permutation.
All inputs are finite; a program needn't handle non-finite values.
Results may differ from a plain program's by a relative error of at most 0.0081.
The roundings to bfloat16 on the way count: a program that leaves them out, or rounds other values in their place, can miss the bound.
Values sent between devices are 32-bit elements; how exact they have to be, the bound alone decides.
A program may use at most 64 MiB of HBM per device.

v0:
```python
import jax
import jax.numpy as jnp
from jax import lax
from jax.sharding import PartitionSpec as P

ITERS = 2


HIGHEST_PRECISION = lax.Precision.HIGHEST


def with_halo(block, sides, width):
    for axis, dim in sides:
        count = lax.axis_size(axis)
        forward = [(i, i + 1) for i in range(count - 1)]
        backward = [(target, source) for source, target in forward]
        low = lax.ppermute(
            lax.slice_in_dim(block, block.shape[dim] - width, None, axis=dim), axis, forward
        )
        high = lax.ppermute(lax.slice_in_dim(block, 0, width, axis=dim), axis, backward)
        block = jnp.concatenate([low, block, high], axis=dim)
    return block


def local(
    applied_loads,
    stiffness,
    local_inverse,
    coarse_basis,
    face_index,
    coarse_map,
    group_inverse,
    top_basis,
    top_inverse,
):
    dev_count = lax.axis_size("dev")
    group_count = lax.axis_size("group")
    dev_pos = lax.axis_index("dev")
    group_pos = lax.axis_index("group")
    dof_count = stiffness.shape[1]
    face_width = dof_count // 4
    rhs_count = applied_loads.shape[2]
    con_count = coarse_basis.shape[1]
    positions = face_index[0]
    stiff_block = stiffness[0]
    inverse_block = local_inverse[0]
    basis_block = coarse_basis[0]
    neighbours = jnp.stack(
        [dev_pos > 0, dev_pos < dev_count - 1, group_pos > 0, group_pos < group_count - 1]
    )
    face_weight = jnp.repeat(jnp.where(neighbours, 0.5, 1.0).astype(jnp.float32), face_width)
    weights = jnp.zeros((dof_count,), jnp.float32).at[positions].set(face_weight)[:, None]
    selector = (coarse_map[0][:, None] == jnp.arange(con_count, dtype=jnp.int32)[None, :]).astype(
        jnp.float32
    )

    def assemble(field):
        face_rows = jnp.take(field, positions, axis=0).reshape(4, face_width, rhs_count)
        along_dev = with_halo(face_rows[0:2], (("dev", 0),), 1)
        along_group = with_halo(face_rows[2:4], (("group", 0),), 1)
        partner = jnp.concatenate(
            [along_dev[0:1], along_dev[3:4], along_group[0:1], along_group[3:4]], axis=0
        )
        return field.at[positions].add(partner.reshape(dof_count, rhs_count))

    def global_sum(left_side, right_side, factor):
        return lax.psum(jnp.sum(factor * left_side * right_side, axis=0), ("group", "dev"))

    def inner_pair(left_side, assembled):
        return global_sum(left_side, assembled, weights)

    def precondition(residual):
        scaled_res = (weights * residual).astype(jnp.bfloat16)
        local_part = jnp.dot(inverse_block, scaled_res, preferred_element_type=jnp.float32)
        coarse_part = jnp.dot(basis_block, scaled_res, preferred_element_type=jnp.float32)
        block_vec = jnp.dot(selector.T, coarse_part, precision=HIGHEST_PRECISION)
        whole_group = lax.all_gather(block_vec, "dev", axis=0, tiled=True)
        solved = jnp.dot(group_inverse, whole_group, precision=HIGHEST_PRECISION)
        reduced = lax.psum(jnp.dot(top_basis.T, block_vec, precision=HIGHEST_PRECISION), "dev")
        stacked = lax.all_gather(reduced, "group", axis=0, tiled=True)
        upper = jnp.dot(top_inverse, stacked, precision=HIGHEST_PRECISION)
        corrected = solved + jnp.dot(top_basis, upper, precision=HIGHEST_PRECISION)
        own_values = jnp.dot(selector, corrected, precision=HIGHEST_PRECISION)
        combined = local_part + jnp.dot(
            basis_block.astype(jnp.float32).T, own_values, precision=HIGHEST_PRECISION
        )
        weighted = weights * combined
        return (assemble(weighted), weighted)

    residual = assemble(applied_loads[0])
    solution = jnp.zeros_like(residual)
    direction, spread_part = precondition(residual)
    norm_now = inner_pair(residual, direction)
    for iteration in range(ITERS):
        product = jnp.dot(
            stiff_block, direction.astype(jnp.bfloat16), preferred_element_type=jnp.float32
        )
        image_vec = assemble(product)
        step_size = norm_now / inner_pair(direction, image_vec)
        solution = solution + step_size * direction
        residual = residual - step_size * image_vec
        precond, spread_part = precondition(residual)
        norm_next = inner_pair(residual, precond)
        direction = precond + norm_next / norm_now * direction
        norm_now = norm_next
    return (solution[None], residual[None], direction[None])


def solution(mesh):
    return jax.shard_map(
        local,
        mesh=mesh,
        in_specs=(
            P(("group", "dev"), None, None),
            P(("group", "dev"), None, None),
            P(("group", "dev"), None, None),
            P(("group", "dev"), None, None),
            P(("group", "dev"), None),
            P(("group", "dev"), None),
            P(("group", "dev"), None),
            P(("group", "dev"), None),
            P("group", None),
        ),
        out_specs=(
            P(("group", "dev"), None, None),
            P(("group", "dev"), None, None),
            P(("group", "dev"), None, None),
        ),
        check_vma=False,
    )
```

profile of v0, /device:TPU:1, one launch (start us, length us, event | category | flops | bytes accessed | tf_op | source)
XLA Modules:
  0.0 858.9 jit_solution(16816099333078481797)
XLA Ops:
  2.6 2.6 gather_fusion
  5.5 4.0 collective-permute-start
  9.5 2.9 collective-permute-start.3
  12.4 3.4 collective-permute-start.2
  15.8 1.3 collective-permute-start.1
  17.3 6.2 scatter_custom_fusion
  23.9 9.1 %scatter_fusion = f32[1536,128]{1,0:T(8,128)S(1)} fusion(f32[1536,128]{1,0:T(8,128)S(1)} %bitcast.147, s32[1536]{0:T(1024)S(1)} %fusion.45, f32[1536,128]{1,0:T(8,128)S(1)} %bitcast.150), kind=kCustom, calls=%fused_computation.7 | custom fusion | flops 196608 | bytes 2365440 | tf_op jit(solution)/shard_map/scatter-add | solution.py:64
  33.6 21.5 %all_gather.18 = f32[768,128]{1,0:T(8,128)S(1)} all-gather(f32[48,128]{1,0:T(8,128)S(1)} %fusion.38), channel_id=1, replica_groups=mesh['group'=16,'dev'=16] {'dev'}, dimensions={0}, use_global_device_ids=true | all-gather | bytes 417792 | tf_op jit(solution)/shard_map/all_gather | solution.py:77
  55.4 58.4 %psum.56 = f32[48,128]{1,0:T(8,128)S(1)} all-reduce(f32[48,128]{1,0:T(8,128)S(1)} %convolution_bitcast_fusion.2), channel_id=1, replica_groups=mesh['group'=16,'dev'=16] {'dev'}, use_global_device_ids=true, to_apply=%region_2.4 | all-reduce | flops 6144 | bytes 49152 | tf_op jit(solution)/shard_map/psum | solution.py:79
  113.8 38.9 %all_gather.19 = f32[768,128]{1,0:T(8,128)S(1)} all-gather(f32[48,128]{1,0:T(8,128)S(1)} %psum.56), channel_id=1, replica_groups=mesh['group'=16,'dev'=16] {'group'}, dimensions={0}, use_global_device_ids=true | all-gather | bytes 417792 | tf_op jit(solution)/shard_map/all_gather | solution.py:80
  153.8 4.3 fusion.8
  158.9 2.6 gather_fusion.1
  161.9 1.3 collective-permute-start.4
  163.2 2.1 collective-permute-start.7
  165.2 3.5 collective-permute-start.6
  168.8 1.3 collective-permute-start.5
  171.3 5.3 collective-permute-done.5
  176.7 9.5 %scatter_fusion.1 = f32[1536,128]{1,0:T(8,128)S(1)} fusion(f32[1536,128]{1,0:T(8,128)S(1)} %copy.33, s32[1536]{0:T(1024)S(1)} %fusion.45, f32[1536,128]{1,0:T(8,128)S(1)} %bitcast.151), kind=kCustom, calls=%fused_computation.8 | custom fusion | flops 196608 | bytes 2365440 | tf_op jit(solution)/shard_map/scatter-add | solution.py:64
  186.2 4.0 fusion.16
  190.5 3.7 gather_fusion.2
  194.2 1.4 broadcast_select_fusion.3
  195.7 1.5 collective-permute-start.8
  197.2 2.0 collective-permute-start.11
  199.2 3.5 collective-permute-start.10
  205.3 5.3 collective-permute-done.9
  210.7 9.1 %scatter_fusion.2 = f32[1536,128]{1,0:T(8,128)S(1)} fusion(f32[1536,128]{1,0:T(8,128)S(1)} %copy.35, s32[1536]{0:T(1024)S(1)} %fusion.45, f32[1536,128]{1,0:T(8,128)S(1)} %bitcast.152), kind=kCustom, calls=%fused_computation.9 | custom fusion | flops 196608 | bytes 2365440 | tf_op jit(solution)/shard_map/scatter-add | solution.py:64
  220.0 74.3 %all-reduce = (f32[128]{0:T(128)S(1)}, f32[128]{0:T(128)S(1)}) all-reduce(f32[128]{0:T(128)S(1)} %get-tuple-element.5, f32[128]{0:T(128)S(1)} %get-tuple-element.4), channel_id=1, replica_groups=mesh['group'=16,'dev'=16] {'group','dev'}, use_global_device_ids=true, to_apply=%region_5.7 | all-reduce | flops 256 | bytes 2048 | tf_op jit(solution)/shard_map/psum | solution.py:67
  295.3 18.1 %all_gather.20 = f32[768,128]{1,0:T(8,128)S(1)} all-gather(f32[48,128]{1,0:T(8,128)S(1)} %fusion.36), channel_id=1, replica_groups=mesh['group'=16,'dev'=16] {'dev'}, dimensions={0}, use_global_device_ids=true | all-gather | bytes 417792 | tf_op jit(solution)/shard_map/all_gather | solution.py:77
  313.4 4.3 fusion.6
  317.7 58.2 %psum.59 = f32[48,128]{1,0:T(8,128)S(1)} all-reduce(f32[48,128]{1,0:T(8,128)S(1)} %convolution_bitcast_fusion.1), channel_id=1, replica_groups=mesh['group'=16,'dev'=16] {'dev'}, use_global_device_ids=true, to_apply=%region_9.11 | all-reduce | flops 6144 | bytes 49152 | tf_op jit(solution)/shard_map/psum | solution.py:79
  376.0 37.1 %all_gather.21 = f32[768,128]{1,0:T(8,128)S(1)} all-gather(f32[48,128]{1,0:T(8,128)S(1)} %psum.59), channel_id=1, replica_groups=mesh['group'=16,'dev'=16] {'group'}, dimensions={0}, use_global_device_ids=true | all-gather | bytes 417792 | tf_op jit(solution)/shard_map/all_gather | solution.py:80
  415.0 1.4 fusion.14
  416.4 1.4 copy.37
  417.8 3.7 gather_fusion.3
  421.5 1.4 broadcast_select_fusion.2
  423.0 1.3 collective-permute-start.12
  424.3 2.1 collective-permute-start.15
  426.4 3.5 collective-permute-start.14
  432.5 5.3 collective-permute-done.13
  437.8 9.1 %scatter_fusion.3 = f32[1536,128]{1,0:T(8,128)S(1)} fusion(f32[1536,128]{1,0:T(8,128)S(1)} %copy.37, s32[1536]{0:T(1024)S(1)} %fusion.45, f32[1536,128]{1,0:T(8,128)S(1)} %bitcast.153), kind=kCustom, calls=%fused_computation.10 | custom fusion | flops 196608 | bytes 2365440 | tf_op jit(solution)/shard_map/scatter-add | solution.py:64
  447.2 72.9 %psum.60 = f32[128]{0:T(128)S(1)} all-reduce(f32[128]{0:T(128)S(1)} %multiply_reduce_fusion.2), channel_id=1, replica_groups=mesh['group'=16,'dev'=16] {'group','dev'}, use_global_device_ids=true, to_apply=%region_12.14 | all-reduce | flops 128 | bytes 1024 | tf_op jit(solution)/shard_map/psum | solution.py:67
  520.1 4.9 fusion.19
  525.0 1.4 copy.39
  526.4 3.7 gather_fusion.4
  530.1 1.4 broadcast_select_fusion.1
  531.6 1.9 collective-permute-start.16
  533.5 2.9 collective-permute-start.19
  536.4 3.6 collective-permute-start.18
  540.0 1.3 collective-permute-start.17
  542.6 5.2 collective-permute-done.17
  548.7 9.4 %scatter_fusion.4 = f32[1536,128]{1,0:T(8,128)S(1)} fusion(f32[1536,128]{1,0:T(8,128)S(1)} %copy.39, s32[1536]{0:T(1024)S(1)} %fusion.45, f32[1536,128]{1,0:T(8,128)} %bitcast.154), kind=kCustom, calls=%fused_computation.11 | custom fusion | flops 196608 | bytes 2365440 | tf_op jit(solution)/shard_map/scatter-add | solution.py:64
  558.5 76.9 %psum.61 = f32[128]{0:T(128)S(1)} all-reduce(f32[128]{0:T(128)S(1)} %multiply_reduce_fusion.1), channel_id=1, replica_groups=mesh['group'=16,'dev'=16] {'group','dev'}, use_global_device_ids=true, to_apply=%region_15.17 | all-reduce | flops 128 | bytes 1024 | tf_op jit(solution)/shard_map/psum | solution.py:67
  636.3 17.7 %all_gather.22 = f32[768,128]{1,0:T(8,128)S(1)} all-gather(f32[48,128]{1,0:T(8,128)S(1)} %fusion.34), channel_id=1, replica_groups=mesh['group'=16,'dev'=16] {'dev'}, dimensions={0}, use_global_device_ids=true | all-gather | bytes 417792 | tf_op jit(solution)/shard_map/all_gather | solution.py:77
  654.1 4.3 fusion.4
  658.4 57.9 %psum.62 = f32[48,128]{1,0:T(8,128)S(1)} all-reduce(f32[48,128]{1,0:T(8,128)S(1)} %convolution_bitcast_fusion), channel_id=1, replica_groups=mesh['group'=16,'dev'=16] {'dev'}, use_global_device_ids=true, to_apply=%region_16.18 | all-reduce | flops 6144 | bytes 49152 | tf_op jit(solution)/shard_map/psum | solution.py:79
  716.3 36.9 %all_gather.23 = f32[768,128]{1,0:T(8,128)S(1)} all-gather(f32[48,128]{1,0:T(8,128)S(1)} %psum.62), channel_id=1, replica_groups=mesh['group'=16,'dev'=16] {'group'}, dimensions={0}, use_global_device_ids=true | all-gather | bytes 417792 | tf_op jit(solution)/shard_map/all_gather | solution.py:80
  756.0 2.6 gather_fusion.5
  758.9 1.3 collective-permute-start.20
  760.3 2.1 collective-permute-start.23
  762.3 3.5 collective-permute-start.22
  765.8 1.3 collective-permute-start.21
  768.4 5.3 collective-permute-done.21
  774.7 9.6 %scatter_fusion.5 = f32[1536,128]{1,0:T(8,128)S(1)} fusion(f32[1536,128]{1,0:T(8,128)S(1)} %copy.41, s32[1536]{0:T(1024)S(1)} %fusion.45, f32[1536,128]{1,0:T(8,128)} %bitcast.149), kind=kCustom, calls=%fused_computation.12 | custom fusion | flops 196608 | bytes 2365440 | tf_op jit(solution)/shard_map/scatter-add | solution.py:64
  784.6 72.7 %psum.63 = f32[128]{0:T(128)S(1)} all-reduce(f32[128]{0:T(128)S(1)} %multiply_reduce_fusion), channel_id=1, replica_groups=mesh['group'=16,'dev'=16] {'group','dev'}, use_global_device_ids=true, to_apply=%region_19.21 | all-reduce | flops 128 | bytes 1024 | tf_op jit(solution)/shard_map/psum | solution.py:67
  (99 shorter events, 26.7 us)
Async XLA Ops:
  0.6 32.3 %copy-start = (bf16[1,48,1536]{2,1,0:T(8,128)(2,1)S(1)}, bf16[1,48,1536]{2,1,0:T(8,128)(2,1)}, u32[]{:S(2)}) copy-start(bf16[1,48,1536]{2,1,0:T(8,128)(2,1)} %param.14) | copy-start | bytes 442372
  2.6 14.7 %copy-start.6 = (s32[1,1536]{1,0:T(1,128)S(1)}, s32[1,1536]{1,0:T(1,128)}, u32[]{:S(2)}) copy-start(s32[1,1536]{1,0:T(1,128)} %param.15) | copy-start | bytes 18436
  5.5 18.0 %collective-permute-start = (f32[1,384,128]{2,1,0:T(8,128)S(1)}, f32[1,384,128]{2,1,0:T(8,128)S(1)}, u32[]{:S(2)}, u32[]{:S(2)}) collective-permute-start(f32[1,384,128]{2,1,0:T(8,128)S(1)} %get-tuple-element.30), channel_id=1, source_target_pairs={{0,1},{1,2},{2,3},{3,4},{4,5},{5,6},{6,7},{7,8},{8,9},{9,10},{10,1... | collective-permute-start | bytes 589832 | tf_op jit(solution)/shard_map/ppermute | solution.py:17
  9.5 14.0 %collective-permute-start.3 = (f32[1,384,128]{2,1,0:T(8,128)S(1)}, f32[1,384,128]{2,1,0:T(8,128)S(1)}, u32[]{:S(2)}, u32[]{:S(2)}) collective-permute-start(f32[1,384,128]{2,1,0:T(8,128)S(1)} %get-tuple-element.31), channel_id=1, source_target_pairs={{16,0},{32,16},{48,32},{64,48},{80,64},{96,80},{112,96},{128,112},... | collective-permute-start | bytes 589832 | tf_op jit(solution)/shard_map/ppermute | solution.py:20
  12.4 11.2 %collective-permute-start.2 = (f32[1,384,128]{2,1,0:T(8,128)S(1)}, f32[1,384,128]{2,1,0:T(8,128)S(1)}, u32[]{:S(2)}, u32[]{:S(2)}) collective-permute-start(f32[1,384,128]{2,1,0:T(8,128)S(1)} %get-tuple-element.32), channel_id=1, source_target_pairs={{0,16},{16,32},{32,48},{48,64},{64,80},{80,96},{96,112},{112,128},... | collective-permute-start | bytes 589832 | tf_op jit(solution)/shard_map/ppermute | solution.py:17
  15.8 8.0 collective-permute-start.1
  23.8 9.5 %copy-start.7 = (s32[1,48]{1,0:T(1,128)S(1)}, s32[1,48]{1,0:T(1,128)}, u32[]{:S(2)}) copy-start(s32[1,48]{1,0:T(1,128)} %param.16) | copy-start | bytes 580
  23.8 31.3 %copy-start.5 = (f32[48,48]{1,0:T(8,128)S(1)}, f32[48,48]{1,0:T(8,128)}, u32[]{:S(2)}) copy-start(f32[48,48]{1,0:T(8,128)} %param.18) | copy-start | bytes 27652
  23.9 128.8 %copy-start.3 = (f32[48,768]{1,0:T(8,128)S(1)}, f32[48,768]{1,0:T(8,128)}, u32[]{:S(2)}) copy-start(f32[48,768]{1,0:T(8,128)} %param.19) | copy-start | bytes 442372
  23.9 129.2 %copy-start.4 = (f32[48,768]{1,0:T(8,128)S(1)}, f32[48,768]{1,0:T(8,128)}, u32[]{:S(2)}) copy-start(f32[48,768]{1,0:T(8,128)} %param.17) | copy-start | bytes 442372
  161.9 8.2 collective-permute-start.4
  163.2 7.0 collective-permute-start.7
  165.2 6.1 collective-permute-start.6
  168.8 7.9 collective-permute-start.5
  195.7 8.4 collective-permute-start.8
  197.2 7.0 collective-permute-start.11
  199.2 6.1 collective-permute-start.10
  202.7 7.9 collective-permute-start.9
  423.0 8.2 collective-permute-start.12
  424.3 7.0 collective-permute-start.15
  426.4 6.1 collective-permute-start.14
  429.9 7.9 collective-permute-start.13
  531.6 9.7 %collective-permute-start.16 = (f32[1,384,128]{2,1,0:T(8,128)S(1)}, f32[1,384,128]{2,1,0:T(8,128)S(1)}, u32[]{:S(2)}, u32[]{:S(2)}) collective-permute-start(f32[1,384,128]{2,1,0:T(8,128)S(1)} %get-tuple-element.14), channel_id=1, source_target_pairs={{0,1},{1,2},{2,3},{3,4},{4,5},{5,6},{6,7},{7,8},{8,9},{9,10},{10,1... | collective-permute-start | bytes 589832 | tf_op jit(solution)/shard_map/ppermute | solution.py:17
  533.5 7.9 collective-permute-start.19
  536.4 6.2 collective-permute-start.18
  540.0 7.8 collective-permute-start.17
  635.4 18.6 %copy-start.1 = (f32[1536,128]{1,0:T(8,128)}, f32[1536,128]{1,0:T(8,128)S(1)}, u32[]{:S(2)}) copy-start(f32[1536,128]{1,0:T(8,128)S(1)} %multiply_subtract_fusion) | copy-start | bytes 2359300
  758.9 8.2 collective-permute-start.20
  760.3 7.0 collective-permute-start.23
  762.3 6.1 collective-permute-start.22
  765.8 7.9 collective-permute-start.21
  774.7 9.7 %copy-start.2 = (f32[1536,128]{1,0:T(8,128)S(1)}, f32[1536,128]{1,0:T(8,128)}, u32[]{:S(2)}) copy-start(f32[1536,128]{1,0:T(8,128)} %copy-done.1) | copy-start | bytes 2359300
where the time goes:
time: 868 us; the launch traced here: 859 us
  blocking collectives  641 us (74%)
  other arithmetic  66.4 us (8%)
  starting transfers between devices  54 us (6%)
  waiting for transfers between devices  33.1 us (4%)
  matrix products  32 us (4%)
  local copies, waits for them, and re-layouts  30.2 us (3%)
    psum x4, blocking collectives, global_sum(): lax.psum(jnp.sum(factor * left_side * right_side, axis=0), ('group', 'dev'))  297 us
    psum x3, blocking collectives, precondition(): lax.psum(jnp.dot(top_basis.T, block_vec, precision=HIGHEST_PRECISION), 'd...  175 us
    all_gather x3, blocking collectives, precondition(): stacked = lax.all_gather(reduced, 'group', axis=0, tiled=True)  113 us
    all_gather x3, blocking collectives, precondition(): whole_group = lax.all_gather(block_vec, 'dev', axis=0, tiled=True)  57.3 us
    scatter-add x6, other arithmetic, assemble(): return field.at[positions].add(partner.reshape(dof_count, rhs_count))  55.8 us
    ppermute x12, starting transfers between devices, with_halo(): lax.ppermute(lax.slice_in_dim(block, block.shape[dim] - width, None, axis...  32.3 us
    ppermute x12, waiting for transfers between devices, with_halo(): lax.ppermute(lax.slice_in_dim(block, 0, width, axis=dim), axis, backward)  27.2 us
    ppermute x12, starting transfers between devices, with_halo(): lax.ppermute(lax.slice_in_dim(block, 0, width, axis=dim), axis, backward)  21.7 us
  transfers between devices with their start and end apart: 24, of which 16 were waited for; matrix products, arithmetic and copies ran while one was open for 1% of the time, Pallas kernels for 0%

commit v1 on v0

v1 whole, which is shorter than its diff:
```python
import functools

import jax
import jax.numpy as jnp
from jax import lax
from jax.experimental import pallas as pl
from jax.experimental.pallas import tpu as pltpu
from jax.sharding import PartitionSpec as P

ITERS = 2
MESH = pl.DeviceIdType.MESH
F32 = jnp.float32
BF16 = jnp.bfloat16
NN = (((1,), (0,)), ((), ()))
NT = (((1,), (1,)), ((), ()))
CHUNK = 128


def dot(a, b, dims=NN):
    return lax.dot_general(a, b, dims, preferred_element_type=F32)


def split(a):
    hi = a.astype(BF16)
    return hi, (a - hi.astype(F32)).astype(BF16)


def dot3(a, b, dims=NN):
    (a_hi, a_lo), (b_hi, b_lo) = a, b
    return dot(a_hi, b_hi, dims) + (dot(a_lo, b_hi, dims) + dot(a_hi, b_lo, dims))


def fold(values):
    rows, cols = values.shape
    return jnp.sum(values.reshape(rows // 8, 8, cols), axis=0)


def main_kernel(
    n_group, n_dev,
    loads_hbm, stiff_hbm, inv_hbm, basis_hbm, pos_smem, pos_row, cmap_row, ginv_ref, tbasis_ref, tinv_ref,
    x_out, r_out, d_out,
    loads, stiff, inv, basis, perm_t,
    field, res, dirn, sol, prod, scaled, scaled_lo, plain,
    face_in, basis_f32, basis_bf, basis_in, comb_t, comb,
    ginv_hi, ginv_lo, tb_hi, tb_lo, tbq_hi, tbq_lo, t2_hi, t2_lo, pad_a, pad_b,
    coarse, u_out, u_in, top_in, ts_in, own, own_in, dot_dev, dot_group,
    load_sem, out_sem, face_send, face_recv, basis_send, basis_recv, own_send, own_recv,
    coarse_send, coarse_recv, u_send, u_recv, top_send, top_recv, ts_send, ts_recv,
    dd_send, dd_recv, dg_send, dg_recv,
):
    g = lax.axis_index("group")
    d = lax.axis_index("dev")
    ni, nrhs = loads.shape
    ncon = basis.shape[0]
    face = ni // 4
    per_dev = nrhs // n_dev
    has = [d > 0, d < n_dev - 1, g > 0, g < n_group - 1]
    target = [(g, d - 1), (g, d + 1), (g - 1, d), (g + 1, d)]
    opposite = [1, 0, 3, 2]
    w = [jnp.where(h, 0.5, 1.0).astype(F32) for h in has]

    def dev_peer(i):
        return (g, lax.rem(d + i, n_dev))

    def group_peer(i):
        return (lax.rem(g + i, n_group), d)

    def fetch(src, dst, k):
        return pltpu.make_async_copy(src, dst, load_sem.at[k])

    fetch_loads = fetch(loads_hbm, loads, 0)
    fetch_basis = fetch(basis_hbm, basis, 1)
    fetch_inv = fetch(inv_hbm, inv, 2)
    fetch_stiff = fetch(stiff_hbm, stiff, 3)
    fetch_loads.start()
    fetch_basis.start()
    fetch_inv.start()
    fetch_stiff.start()

    barrier = pltpu.get_barrier_semaphore()

    def greet_dev(i, carry):
        pl.semaphore_signal(barrier, inc=1, device_id=dev_peer(i), device_id_type=MESH)
        return carry

    def greet_group(i, carry):
        pl.semaphore_signal(barrier, inc=1, device_id=group_peer(i), device_id_type=MESH)
        return carry

    lax.fori_loop(1, n_dev, greet_dev, 0)
    lax.fori_loop(1, n_group, greet_group, 0)

    def spread(src_of, buf, k, send, recv, along_dev):
        n, me = (n_dev, d) if along_dev else (n_group, g)
        peer_of = dev_peer if along_dev else group_peer

        def body(i, carry):
            peer = peer_of(i)
            pltpu.make_async_remote_copy(
                src_ref=src_of(peer[1] if along_dev else peer[0]),
                dst_ref=buf.at[k, me],
                send_sem=send.at[k],
                recv_sem=recv.at[k],
                device_id=peer,
                device_id_type=MESH,
            ).start()
            return carry

        lax.fori_loop(1, n, body, 0)

    def all_of(buf, k, send, recv, along_dev):
        n = n_dev if along_dev else n_group
        part = buf.at[k, pl.ds(0, n - 1)]
        return pltpu.make_async_remote_copy(
            src_ref=part, dst_ref=part, send_sem=send.at[k], recv_sem=recv.at[k],
            device_id=dev_peer(1) if along_dev else group_peer(1), device_id_type=MESH,
        )

    def face_copy(src, e, b):
        return pltpu.make_async_remote_copy(
            src_ref=src.at[pl.ds(b * face, face)], dst_ref=face_in.at[e, opposite[b]],
            send_sem=face_send.at[e, b], recv_sem=face_recv.at[e, opposite[b]],
            device_id=target[b], device_id_type=MESH,
        )

    def face_wait(src, e, b):
        return pltpu.make_async_remote_copy(
            src_ref=src.at[pl.ds(b * face, face)], dst_ref=face_in.at[e, b],
            send_sem=face_send.at[e, b], recv_sem=face_recv.at[e, b],
            device_id=target[b], device_id_type=MESH,
        )

    def send_face(src, e, b):
        @pl.when(has[b])
        def _():
            face_copy(src, e, b).start()

    def recv_face(src, e, b):
        @pl.when(has[b])
        def _():
            face_wait(src, e, b).wait_recv()

    def sent_face(src, e, b):
        @pl.when(has[b])
        def _():
            face_copy(src, e, b).wait_send()

    def basis_copy(b):
        return pltpu.make_async_remote_copy(
            src_ref=basis_f32.at[:, pl.ds(b * face, face)], dst_ref=basis_in.at[opposite[b]],
            send_sem=basis_send.at[b], recv_sem=basis_recv.at[opposite[b]],
            device_id=target[b], device_id_type=MESH,
        )

    def basis_wait(b):
        return pltpu.make_async_remote_copy(
            src_ref=basis_f32.at[:, pl.ds(b * face, face)], dst_ref=basis_in.at[b],
            send_sem=basis_send.at[b], recv_sem=basis_recv.at[b],
            device_id=target[b], device_id_type=MESH,
        )

    def own_copy(m, b):
        return pltpu.make_async_remote_copy(
            src_ref=own.at[m], dst_ref=own_in.at[m, opposite[b]],
            send_sem=own_send.at[m, b], recv_sem=own_recv.at[m, opposite[b]],
            device_id=target[b], device_id_type=MESH,
        )

    def own_wait(m, b):
        return pltpu.make_async_remote_copy(
            src_ref=own.at[m], dst_ref=own_in.at[m, b],
            send_sem=own_send.at[m, b], recv_sem=own_recv.at[m, b],
            device_id=target[b], device_id_type=MESH,
        )

    def gather_face(src, dst, b):
        def body(step, carry):
            base = b * face + step * 16
            for j in range(16):
                row = pos_smem[0, base + j]
                dst[pl.ds(base + j, 1), :] = src[pl.ds(row, 1), :]
            return carry

        lax.fori_loop(0, face // 16, body, 0)

    def over_face(b, body, init):
        def step(i, carry):
            return body(pl.ds(pl.multiple_of(b * face + i * CHUNK, CHUNK), CHUNK),
                        pl.ds(pl.multiple_of(i * CHUNK, CHUNK), CHUNK), carry)

        return lax.fori_loop(0, face // CHUNK, step, init)

    def apply(matrix, vector, out, out_type):
        rows = 512 if ni % 512 == 0 else ni

        def body(i, carry):
            at = pl.ds(pl.multiple_of(i * rows, rows), rows)
            out[at, :] = dot(matrix[at, :], vector[...]).astype(out_type)
            return carry

        lax.fori_loop(0, ni // rows, body, 0)

    for b in range(4):
        @pl.when(jnp.logical_not(has[b]))
        def _():
            def zero(e, carry):
                face_in[e, b] = jnp.zeros((face, nrhs), F32)
                return carry

            lax.fori_loop(0, face_in.shape[0], zero, 0)
            for m in range(ITERS + 1):
                own_in[m, b] = jnp.zeros((ncon, nrhs), F32)
            basis_in[b] = jnp.zeros((ncon, face), F32)

    fetch_loads.wait()
    gather_face(loads, field, 0)
    gather_face(loads, field, 1)
    pl.semaphore_wait(barrier, n_dev - 1 + n_group - 1)
    send_face(field, 0, 0)
    send_face(field, 0, 1)
    gather_face(loads, field, 2)
    send_face(field, 0, 2)
    gather_face(loads, field, 3)
    send_face(field, 0, 3)

    def build(i, carry):
        rows = lax.broadcasted_iota(jnp.int32, (CHUNK, ni), 0) + i * CHUNK
        at = pl.ds(pl.multiple_of(i * CHUNK, CHUNK), CHUNK)
        perm_t[at, :] = jnp.where(rows == pos_row[...], 1.0, 0.0).astype(BF16)
        return carry

    lax.fori_loop(0, ni // CHUNK, build, 0)

    select = jnp.where(
        lax.broadcasted_iota(jnp.int32, (ncon, ncon), 0) == cmap_row[...], 1.0, 0.0
    ).astype(BF16)
    fetch_basis.wait()
    ordered = dot(select, basis[...]).astype(BF16)
    width = 512 if ni % 512 == 0 else ni
    for j in range(ni // width):
        block = dot(ordered, perm_t[:, j * width:(j + 1) * width])
        basis_f32[:, j * width:(j + 1) * width] = block
        basis_bf[:, j * width:(j + 1) * width] = block.astype(BF16)
    for b in range(4):
        @pl.when(has[b])
        def _():
            basis_copy(b).start()

    ginv_hi[...], ginv_lo[...] = split(ginv_ref[...])
    topc = tbasis_ref.shape[1]
    pad_a[...] = jnp.zeros_like(pad_a)
    pad_a[0:ncon, 0:topc] = tbasis_ref[...]
    tb_hi[...], tb_lo[...] = split(pad_a[...])
    mark_row = lax.broadcasted_iota(jnp.int32, (64, 128), 0)
    mark_col = lax.broadcasted_iota(jnp.int32, (64, 128), 1)
    marked = jnp.where((mark_row == ncon) & (mark_col == 64), 1.0, pad_a[0:64, :])
    tbq_hi[...], tbq_lo[...] = split(marked)
    pad_b[...] = jnp.zeros_like(pad_b)
    pad_b[0:topc, 0:n_group * topc] = tinv_ref[...]
    t2_hi[...] = jnp.zeros_like(t2_hi)
    t2_lo[...] = jnp.zeros_like(t2_lo)
    for q in range(n_group):
        tinv_t = pad_b[:, (q * topc) // 128 * 128:((q * topc) // 128 + 2) * 128].T
        start = (q * topc) % 128
        hi, lo = split(tinv_t[start:start + topc])
        at = (q // 2) * 128 + (q % 2) * 64
        t2_hi[at:at + topc, :] = hi
        t2_lo[at:at + topc, :] = lo

    for b in range(4):
        recv_face(field, 0, b)

        def add(at, at_in, carry):
            value = field[at, :] + face_in[0, b, at_in, :]
            res[at, :] = value
            scaled[at, :] = (w[b] * value).astype(BF16)
            scaled_lo[at, :] = (w[b] * value - (w[b] * value).astype(BF16).astype(F32)).astype(BF16)
            return carry

        over_face(b, add, 0)

    odd = lax.rem(g, 2) == 1

    def precondition(m, e, before_end):
        own_coarse = dot(basis_bf[...], scaled[...])
        coarse[m, d] = own_coarse
        pad_a[0:ncon, :] = own_coarse
        u_t = dot3(split(pad_a[...].T), (tb_hi[...], tb_lo[...]))
        u_out[m] = u_t.reshape(n_dev, per_dev, 128)
        u_in[m, d] = u_out[m, d]
        spread(lambda p: u_out.at[m, p], u_in, m, u_send, u_recv, True)
        spread(lambda p: coarse.at[m, d], coarse, m, coarse_send, coarse_recv, True)

        apply(perm_t, scaled, plain, BF16)
        exact_coarse = own_coarse + dot(basis_bf[...], scaled_lo[...])

        all_of(u_in, m, u_send, u_recv, True).wait_recv()
        top = jnp.sum(u_in[m], axis=0)
        top_in[m, g] = jnp.where(odd, pltpu.roll(top, 64, 1), top)
        spread(lambda p: top_in.at[m, g], top_in, m, top_send, top_recv, False)

        if m == 0:
            fetch_inv.wait()
        apply(inv, plain, prod, F32)
        for b in range(4):
            gather_face(prod, field, b)
            send_face(field, e, b)

        all_of(top_in, m, top_send, top_recv, False).wait_recv()
        every = top_in[m]
        joined = jnp.concatenate(
            [every[2 * q] + every[2 * q + 1] for q in range(n_group // 2)], axis=1
        )
        ts = dot3(split(joined), (t2_hi[...], t2_lo[...]))
        energy = jnp.sum(ts * top, axis=1, keepdims=True)
        lane = lax.broadcasted_iota(jnp.int32, ts.shape, 1)
        ts_in[m, d] = jnp.where(lane == 64, energy, ts)
        spread(lambda p: ts_in.at[m, d], ts_in, m, ts_send, ts_recv, True)

        total = jnp.zeros((8, nrhs), F32)
        for b in range(4):
            def part(at, at_in, carry):
                return carry + fold(res[at, :] * field[at, :])

            total = total + w[b] * over_face(b, part, jnp.zeros((8, nrhs), F32))

        all_of(coarse, m, coarse_send, coarse_recv, True).wait_recv()
        solved = dot3((ginv_hi[...], ginv_lo[...]), split(coarse[m].reshape(n_dev * ncon, nrhs)))
        k = m
        dot_dev[k, d] = total + fold(exact_coarse * solved)
        spread(lambda p: dot_dev.at[k, d], dot_dev, k, dd_send, dd_recv, True)

        all_of(ts_in, m, ts_send, ts_recv, True).wait_recv()
        upper = dot3((tbq_hi[...], tbq_lo[...]), split(ts_in[m].reshape(nrhs, 128)), NT)
        own[m] = solved + upper[0:ncon]
        for b in range(4):
            @pl.when(has[b])
            def _():
                own_copy(m, b).start()

        all_of(dot_dev, k, dd_send, dd_recv, True).wait_recv()
        row = lax.broadcasted_iota(jnp.int32, (8, nrhs), 0)
        dot_group[k, g] = jnp.sum(dot_dev[k], axis=0) + jnp.where(
            row == 0, upper[ncon:ncon + 1], 0.0
        )
        spread(lambda p: dot_group.at[k, g], dot_group, k, dg_send, dg_recv, False)

        before_end()

        own_hi, own_lo = split(own[m])
        for b in range(4):
            @pl.when(has[b])
            def _():
                own_wait(m, b).wait_recv()

            recv_face(field, e, b)
            in_hi, in_lo = split(own_in[m, b])
            values = jnp.concatenate(
                [own_hi, in_hi, own_lo, in_lo, jnp.zeros((256 - 4 * ncon, nrhs), BF16)], axis=0
            )

            def join(at, at_in, carry):
                prod[at, :] = w[b] * (
                    field[at, :] + face_in[e, b, at_in, :] + dot(comb[at, :], values)
                )
                return carry

            over_face(b, join, 0)

        all_of(dot_group, k, dg_send, dg_recv, False).wait_recv()
        return jnp.sum(jnp.sum(dot_group[k], axis=0), axis=0, keepdims=True)

    def drain(m, e):
        all_of(u_in, m, u_send, u_recv, True).wait_send()
        all_of(coarse, m, coarse_send, coarse_recv, True).wait_send()
        all_of(top_in, m, top_send, top_recv, False).wait_send()
        all_of(ts_in, m, ts_send, ts_recv, True).wait_send()
        all_of(dot_dev, m, dd_send, dd_recv, True).wait_send()
        all_of(dot_group, m, dg_send, dg_recv, False).wait_send()
        for b in range(4):
            @pl.when(has[b])
            def _():
                own_copy(m, b).wait_send()

            sent_face(field, e, b)

    for b in range(4):
        sent_face(field, 0, b)
    pad_a[...] = jnp.zeros_like(pad_a)

    def combine():
        for b in range(4):
            @pl.when(has[b])
            def _():
                basis_wait(b).wait_recv()

            at = slice(b * face, (b + 1) * face)
            comb_t[0:ncon, at] = basis_f32[:, at]
            comb_t[ncon:2 * ncon, at] = basis_in[b]
            comb_t[2 * ncon:3 * ncon, at] = basis_f32[:, at]
            comb_t[3 * ncon:4 * ncon, at] = basis_in[b]
        comb_t[4 * ncon:, :] = jnp.zeros((256 - 4 * ncon, ni), F32)
        for j in range(ni // 128):
            comb[j * 128:(j + 1) * 128, :] = comb_t[:, j * 128:(j + 1) * 128].T.astype(BF16)
        for b in range(4):
            @pl.when(has[b])
            def _():
                basis_copy(b).wait_send()

    norm = precondition(0, 1, combine)

    def first(i, carry):
        at = pl.ds(pl.multiple_of(i * CHUNK, CHUNK), CHUNK)
        value = prod[at, :]
        dirn[at, :] = value
        scaled[at, :] = value.astype(BF16)
        return carry

    lax.fori_loop(0, ni // CHUNK, first, 0)
    drain(0, 1)

    fetch_stiff.wait()
    for it in range(ITERS):
        e = 2 + 2 * it
        k = ITERS + 1 + it
        apply(perm_t, scaled, plain, BF16)
        apply(stiff, plain, prod, F32)
        for b in range(4):
            gather_face(prod, field, b)
            send_face(field, e, b)

        def part(i, carry):
            at = pl.ds(pl.multiple_of(i * CHUNK, CHUNK), CHUNK)
            return carry + fold(dirn[at, :] * field[at, :])

        dot_dev[k, d] = lax.fori_loop(0, ni // CHUNK, part, jnp.zeros((8, nrhs), F32))
        spread(lambda p: dot_dev.at[k, d], dot_dev, k, dd_send, dd_recv, True)
        all_of(dot_dev, k, dd_send, dd_recv, True).wait_recv()
        dot_group[k, g] = jnp.sum(dot_dev[k], axis=0)
        spread(lambda p: dot_group.at[k, g], dot_group, k, dg_send, dg_recv, False)
        all_of(dot_group, k, dg_send, dg_recv, False).wait_recv()
        curvature = jnp.sum(jnp.sum(dot_group[k], axis=0), axis=0, keepdims=True)
        step_size = norm / curvature

        for b in range(4):
            recv_face(field, e, b)

            def update(at, at_in, carry):
                image = field[at, :] + face_in[e, b, at_in, :]
                value = res[at, :] - step_size * image
                res[at, :] = value
                weighted = w[b] * value
                rounded = weighted.astype(BF16)
                scaled[at, :] = rounded
                scaled_lo[at, :] = (weighted - rounded.astype(F32)).astype(BF16)
                return carry

            over_face(b, update, 0)
        for b in range(4):
            sent_face(field, e, b)

        def after(it=it, step_size=step_size):
            def body(i, carry):
                at = pl.ds(pl.multiple_of(i * CHUNK, CHUNK), CHUNK)
                add = step_size * dirn[at, :]
                sol[at, :] = add if it == 0 else sol[at, :] + add
                return carry

            lax.fori_loop(0, ni // CHUNK, body, 0)
            if it == ITERS - 1:
                pltpu.make_async_copy(sol, x_out, out_sem.at[0]).start()
                pltpu.make_async_copy(res, r_out, out_sem.at[1]).start()

        norm_next = precondition(it + 1, e + 1, after)
        ratio = norm_next / norm

        def turn(i, carry):
            at = pl.ds(pl.multiple_of(i * CHUNK, CHUNK), CHUNK)
            value = prod[at, :] + ratio * dirn[at, :]
            dirn[at, :] = value
            scaled[at, :] = value.astype(BF16)
            return carry

        lax.fori_loop(0, ni // CHUNK, turn, 0)
        norm = norm_next
        if it == ITERS - 1:
            pltpu.make_async_copy(dirn, d_out, out_sem.at[2]).start()
        all_of(dot_dev, k, dd_send, dd_recv, True).wait_send()
        all_of(dot_group, k, dg_send, dg_recv, False).wait_send()
        drain(it + 1, e + 1)

    pltpu.make_async_copy(sol, x_out, out_sem.at[0]).wait()
    pltpu.make_async_copy(res, r_out, out_sem.at[1]).wait()
    pltpu.make_async_copy(dirn, d_out, out_sem.at[2]).wait()


def reorder_kernel(pos_smem, x_in, r_in, d_in, x_out, r_out, d_out):
    def body(step, carry):
        for j in range(8):
            at = step * 8 + j
            row = pos_smem[0, at]
            x_out[pl.ds(row, 1), :] = x_in[pl.ds(at, 1), :]
            r_out[pl.ds(row, 1), :] = r_in[pl.ds(at, 1), :]
            d_out[pl.ds(row, 1), :] = d_in[pl.ds(at, 1), :]
        return carry

    lax.fori_loop(0, x_in.shape[0] // 8, body, 0)


def local(
    n_group, n_dev,
    applied_loads, stiffness, local_inverse, coarse_basis, face_index, coarse_map, group_inverse, top_basis, top_inverse,
):
    ni, nrhs = applied_loads.shape[1:]
    ncon = coarse_basis.shape[1]
    topc = top_basis.shape[1]
    face = ni // 4
    per_dev = nrhs // n_dev
    uses = ITERS + 1
    dots = 2 * ITERS + 1
    exchanges = 2 * ITERS + 2
    top_cols = n_group // 2 * 128
    top_pad = (n_group * topc + 127) // 128 * 128 + 128
    vmem = pl.BlockSpec(memory_space=pltpu.VMEM)
    smem = pl.BlockSpec(memory_space=pltpu.SMEM)
    hbm = pl.BlockSpec(memory_space=pl.ANY)
    field = jax.ShapeDtypeStruct((ni, nrhs), F32)
    dma = pltpu.SemaphoreType.DMA
    scratch = [
        pltpu.VMEM((ni, nrhs), F32), pltpu.VMEM((ni, ni), BF16), pltpu.VMEM((ni, ni), BF16),
        pltpu.VMEM((ncon, ni), BF16), pltpu.VMEM((ni, ni), BF16),
        pltpu.VMEM((ni, nrhs), F32), pltpu.VMEM((ni, nrhs), F32), pltpu.VMEM((ni, nrhs), F32),
        pltpu.VMEM((ni, nrhs), F32), pltpu.VMEM((ni, nrhs), F32),
        pltpu.VMEM((ni, nrhs), BF16), pltpu.VMEM((ni, nrhs), BF16), pltpu.VMEM((ni, nrhs), BF16),
        pltpu.VMEM((exchanges, 4, face, nrhs), F32),
        pltpu.VMEM((ncon, ni), F32), pltpu.VMEM((ncon, ni), BF16), pltpu.VMEM((4, ncon, face), F32),
        pltpu.VMEM((256, ni), F32), pltpu.VMEM((ni, 256), BF16),
        pltpu.VMEM((ncon, n_dev * ncon), BF16), pltpu.VMEM((ncon, n_dev * ncon), BF16),
        pltpu.VMEM((128, 128), BF16), pltpu.VMEM((128, 128), BF16),
        pltpu.VMEM((64, 128), BF16), pltpu.VMEM((64, 128), BF16),
        pltpu.VMEM((top_cols, 128), BF16), pltpu.VMEM((top_cols, 128), BF16),
        pltpu.VMEM((128, 128), F32), pltpu.VMEM((128, top_pad), F32),
        pltpu.VMEM((uses, n_dev, ncon, nrhs), F32),
        pltpu.VMEM((uses, n_dev, per_dev, 128), F32), pltpu.VMEM((uses, n_dev, per_dev, 128), F32),
        pltpu.VMEM((uses, n_group, per_dev, 128), F32),
        pltpu.VMEM((uses, n_dev, per_dev, 128), F32),
        pltpu.VMEM((uses, ncon, nrhs), F32), pltpu.VMEM((uses, 4, ncon, nrhs), F32),
        pltpu.VMEM((dots, n_dev, 8, nrhs), F32), pltpu.VMEM((dots, n_group, 8, nrhs), F32),
        dma((4,)), dma((3,)),
        dma((exchanges, 4)), dma((exchanges, 4)), dma((4,)), dma((4,)), dma((uses, 4)), dma((uses, 4)),
        dma((uses,)), dma((uses,)), dma((uses,)), dma((uses,)),
        dma((uses,)), dma((uses,)), dma((uses,)), dma((uses,)),
        dma((dots,)), dma((dots,)), dma((dots,)), dma((dots,)),
    ]
    x, r, dirn = pl.pallas_call(
        functools.partial(main_kernel, n_group, n_dev),
        out_shape=[field] * 3,
        in_specs=[hbm, hbm, hbm, hbm, smem, vmem, vmem, vmem, vmem, vmem],
        out_specs=[hbm] * 3,
        scratch_shapes=scratch,
        compiler_params=pltpu.CompilerParams(
            collective_id=0, has_side_effects=True, vmem_limit_bytes=56 * 2**20
        ),
        cost_estimate=pl.CostEstimate(
            flops=18 * ni * ni * nrhs, bytes_accessed=4 * ni * ni + 24 * ni * nrhs, transcendentals=0
        ),
        name="pcg",
    )(
        applied_loads[0], stiffness[0], local_inverse[0], coarse_basis[0],
        face_index, face_index, coarse_map, group_inverse, top_basis, top_inverse,
    )
    x, r, dirn = pl.pallas_call(
        reorder_kernel,
        out_shape=[field] * 3,
        in_specs=[smem, vmem, vmem, vmem],
        out_specs=[vmem] * 3,
        compiler_params=pltpu.CompilerParams(vmem_limit_bytes=32 * 2**20),
        cost_estimate=pl.CostEstimate(flops=0, bytes_accessed=24 * ni * nrhs, transcendentals=0),
        name="to_subdomain_order",
    )(face_index, x, r, dirn)
    return x[None], r[None], dirn[None]


def solution(mesh):
    both = ("group", "dev")
    return jax.shard_map(
        functools.partial(local, mesh.shape["group"], mesh.shape["dev"]),
        mesh=mesh,
        in_specs=(
            P(both, None, None), P(both, None, None), P(both, None, None), P(both, None, None),
            P(both, None), P(both, None), P(both, None), P(both, None), P("group", None),
        ),
        out_specs=(P(both, None, None),) * 3,
        check_vma=False,
    )
```

time: 868 us -> 134 us (0.15); the launches traced: 859 us -> 134 us
  blocking collectives: 641 us -> 0 us
  Pallas kernels: 0 us -> 130 us
  other arithmetic: 66.4 us -> 0 us
  starting transfers between devices: 54 us -> 0 us
  waiting for transfers between devices: 33.1 us -> 0 us
  matrix products: 32 us -> 0 us
  local copies, waits for them, and re-layouts: 30.2 us -> 3.4 us
    psum x7 -> x0, blocking collectives: 471 us -> none  [the longest x4 297 us: global_sum(): lax.psum(jnp.sum(factor * left_side * right_side, axis=0), ('group', 'dev'))]
    all_gather x6 -> x0, blocking collectives: 170 us -> none  [the longest x3 113 us: precondition(): stacked = lax.all_gather(reduced, 'group', axis=0, tiled=True)]
    pallas_call x0 -> x2, Pallas kernels: none -> 130 us  [the longest x1 125 us: local(): pl.pallas_call(functools.partial(main_kernel, n_group, n_dev), out_shape=...]
    scatter-add x6 -> x0, other arithmetic: 55.8 us -> none  [assemble(): return field.at[positions].add(partner.reshape(dof_count, rhs_count))]
    ppermute x24 -> x0, starting transfers between devices: 54 us -> none  [the longest x12 32.3 us: with_halo(): lax.ppermute(lax.slice_in_dim(block, block.shape[dim] - width, None, axis...]
    ppermute x24 -> x0, waiting for transfers between devices: 33.1 us -> none  [the longest x12 27.2 us: with_halo(): lax.ppermute(lax.slice_in_dim(block, 0, width, axis=dim), axis, backward)]
    dot_general x29 -> x0, matrix products: 32 us -> none  [the longest x3 13 us: precondition(): jnp.dot(inverse_block, scaled_res, preferred_element_type=jnp.float32)]
    gather x6 -> x0, local copies, waits for them, and re-layouts: 18.9 us -> none  [assemble(): jnp.take(field, positions, axis=0).reshape(4, face_width, rhs_count)]
  transfers between devices with their start and end apart: 24 -> 0, of which waited for: 16 -> 0; matrix products, arithmetic and copies ran while one was open for 1% -> 0% of each run, Pallas kernels for 0% -> 0%
where the time goes in v1:
time: 134 us
  Pallas kernels  130 us (97%)
  local copies, waits for them, and re-layouts  3.4 us (3%)
    pallas_call x1, Pallas kernels, local(): pl.pallas_call(functools.partial(main_kernel, n_group, n_dev), out_shape=...  125 us
    pallas_call x1, Pallas kernels, local(): pl.pallas_call(reorder_kernel, out_shape=[field] * 3, in_specs=[smem, vme...  4.96 us
    unnamed x8, local copies, waits for them, and re-layouts  3.4 us

profile of v1, /device:TPU:1, one launch (start us, length us, event | category | flops | bytes accessed | tf_op | source)
XLA Modules:
  0.0 133.8 jit_solution(8604692214795276116)
XLA Ops:
  0.6 0.0 copy-start.3
  0.6 124.8 %pcg.1 = (f32[1536,128]{1,0:T(8,128)}, f32[1536,128]{1,0:T(8,128)}, f32[1536,128]{1,0:T(8,128)}) custom-call(f32[1536,128]{1,0:T(8,128)} %bitcast.9, bf16[1536,1536]{1,0:T(8,128)(2,1)} %bitcast.7, bf16[1536,1536]{1,0:T(8,128)(2,1)} %bitcast.8, bf16[48,1536]{1,0:T(8,128)(2,1)} %bitcast.13, s32[1,1536]{1,0:T(1,128)} %pos_smem.3, s32[1,1536]{1,0:T(1,128)} %pos_smem.3, ...), custom_call_target="tpu_custom_call" | custom-call | flops 5435817984 | bytes 14155776 | tf_op jit(solution)/shard_map/pcg/pallas_call | solution.py:555
  125.5 0.0 copy-done.3
  125.5 0.0 copy-start
  125.5 1.1 copy-done
  126.6 0.0 copy-start.1
  126.6 1.1 copy-done.1
  127.7 0.0 copy-start.2
  127.7 1.1 copy-done.2
  128.9 5.0 %to_subdomain_order.1 = (f32[1536,128]{1,0:T(8,128)}, f32[1536,128]{1,0:T(8,128)}, f32[1536,128]{1,0:T(8,128)}) custom-call(s32[1,1536]{1,0:T(1,128)S(1)} %copy-done.3, f32[1536,128]{1,0:T(8,128)S(1)} %copy-done, f32[1536,128]{1,0:T(8,128)S(1)} %copy-done.1, f32[1536,128]{1,0:T(8,128)S(1)} %copy-done.2), custom_call_target="tpu_custom_call" | custom-call | bytes 4718592 | tf_op jit(solution)/shard_map/to_subdomain_order/pallas_call | solution.py:572
Async XLA Ops:
  0.6 124.8 %copy-start.3 = (s32[1,1536]{1,0:T(1,128)S(1)}, s32[1,1536]{1,0:T(1,128)}, u32[]{:S(2)}) copy-start(s32[1,1536]{1,0:T(1,128)} %pos_smem.3) | copy-start | bytes 18436
  125.5 1.1 copy-start
  126.6 1.1 copy-start.1
  127.7 1.1 copy-start.2

commit v2 on v0

v2 whole, which is shorter than its diff:
```python
import functools

import jax
import jax.numpy as jnp
from jax import lax
from jax.experimental import pallas as pl
from jax.experimental.pallas import tpu as pltpu
from jax.sharding import PartitionSpec as P

ITERS = 2
MESH = pl.DeviceIdType.MESH
F32 = jnp.float32
BF16 = jnp.bfloat16
NN = (((1,), (0,)), ((), ()))
NT = (((1,), (1,)), ((), ()))
CHUNK = 128
ROWS = 512


def dot(a, b, dims=NN):
    return lax.dot_general(a, b, dims, preferred_element_type=F32)


def split(a):
    hi = a.astype(BF16)
    return hi, (a - hi.astype(F32)).astype(BF16)


def dot3(a, b, dims=NN):
    (a_hi, a_lo), (b_hi, b_lo) = a, b
    return dot(a_hi, b_hi, dims) + (dot(a_lo, b_hi, dims) + dot(a_hi, b_lo, dims))


def fold(values):
    rows, cols = values.shape
    return jnp.sum(values.reshape(rows // 8, 8, cols), axis=0)


def main_kernel(
    n_group, n_dev,
    loads_hbm, stiff_hbm, inv_hbm, basis_hbm, pos_smem, pos_row, cmap_row, ginv_ref, tbasis_ref, tinv_ref,
    x_out, r_out, d_out, one_out,
    loads, stiff, inv, basis, perm_t, place_vec, place_smem,
    field, local_part, res, dirn, sol, prod, weighted, scaled, scaled_lo, plain,
    face_in, basis_f32, basis_in, basis_all, comb_t, comb,
    ginv_hi, ginv_lo, tb_all, tb_all_hi, tb_all_lo, t2_hi, t2_lo, tinv_all, turned,
    tb_own, tb_in, tinv_own, tinv_in, upper,
    parts, parts_in, coarse, u_out, u_in, top_in, ts_in, solved_own, solved_in,
    group_now, top_now, step_now, step_cols, norm_now, dot_dev, dot_group, curv_dev, curv_group,
    load_sem, out_sem, face_send, face_recv, basis_send, basis_recv, tb_send, tb_recv,
    tinv_send, tinv_recv, parts_send, parts_recv, solved_send, solved_recv,
    coarse_send, coarse_recv, u_send, u_recv, top_send, top_recv, ts_send, ts_recv,
    dd_send, dd_recv, dg_send, dg_recv, cd_send, cd_recv, cg_send, cg_recv,
):
    g = lax.axis_index("group")
    d = lax.axis_index("dev")
    ni, nrhs = loads.shape
    ncon = basis.shape[0]
    topc = tbasis_ref.shape[1]
    face = ni // 4
    per_dev = nrhs // n_dev
    has = [d > 0, d < n_dev - 1, g > 0, g < n_group - 1]
    target = [(g, d - 1), (g, d + 1), (g - 1, d), (g + 1, d)]
    opposite = [1, 0, 3, 2]
    w = [jnp.where(h, 0.5, 1.0).astype(F32) for h in has]

    def weight_of(b):
        return jnp.where(b == 0, w[0], jnp.where(b == 1, w[1], jnp.where(b == 2, w[2], w[3])))

    def dev_peer(i):
        return (g, lax.rem(d + i, n_dev))

    def group_peer(i):
        return (lax.rem(g + i, n_group), d)

    def fetch(src, dst, k):
        return pltpu.make_async_copy(src, dst, load_sem.at[k])

    fetch_loads = fetch(loads_hbm, loads, 0)
    fetch_basis = fetch(basis_hbm, basis, 1)
    fetch_inv = fetch(inv_hbm, inv, 2)
    fetch_stiff = fetch(stiff_hbm, stiff, 3)
    fetch_basis.start()
    fetch_loads.start()
    one_out[...] = jnp.ones_like(one_out)

    barrier = pltpu.get_barrier_semaphore()

    def greet_dev(i, carry):
        pl.semaphore_signal(barrier, inc=1, device_id=dev_peer(i), device_id_type=MESH)
        return carry

    def greet_group(i, carry):
        pl.semaphore_signal(barrier, inc=1, device_id=group_peer(i), device_id_type=MESH)
        return carry

    lax.fori_loop(1, n_dev, greet_dev, 0)
    lax.fori_loop(1, n_group, greet_group, 0)

    def spread(src_of, buf, k, send, recv, along_dev):
        n, me = (n_dev, d) if along_dev else (n_group, g)
        peer_of = dev_peer if along_dev else group_peer

        def body(i, carry):
            peer = peer_of(i)
            pltpu.make_async_remote_copy(
                src_ref=src_of(peer[1] if along_dev else peer[0]),
                dst_ref=buf.at[k, me],
                send_sem=send.at[k],
                recv_sem=recv.at[k],
                device_id=peer,
                device_id_type=MESH,
            ).start()
            return carry

        lax.fori_loop(1, n, body, 0)

    def all_of(buf, k, send, recv, along_dev):
        n = n_dev if along_dev else n_group
        part = buf.at[k, pl.ds(0, n - 1)]
        return pltpu.make_async_remote_copy(
            src_ref=part, dst_ref=part, send_sem=send.at[k], recv_sem=recv.at[k],
            device_id=dev_peer(1) if along_dev else group_peer(1), device_id_type=MESH,
        )

    def neighbour_copy(src, dst, send, recv, b):
        return pltpu.make_async_remote_copy(
            src_ref=src, dst_ref=dst, send_sem=send, recv_sem=recv,
            device_id=target[b], device_id_type=MESH,
        )

    def face_copy(src, e, b, slot):
        return neighbour_copy(
            src.at[pl.ds(b * face, face)], face_in.at[e, slot], face_send.at[e, b], face_recv.at[e, slot], b
        )

    def basis_copy(b, slot):
        return neighbour_copy(
            basis_f32.at[:, pl.ds(b * face, face)], basis_in.at[slot], basis_send.at[b], basis_recv.at[slot], b
        )

    def tb_copy(b, slot):
        return neighbour_copy(tb_own, tb_in.at[slot], tb_send.at[b], tb_recv.at[slot], b)

    def tinv_copy(b, slot):
        return neighbour_copy(tinv_own, tinv_in.at[slot - 2], tinv_send.at[b - 2], tinv_recv.at[slot - 2], b)

    def parts_copy(m, b, slot):
        return neighbour_copy(
            parts.at[m, pl.ds((b + 1) * ncon, ncon)], parts_in.at[m, slot],
            parts_send.at[m, b], parts_recv.at[m, slot], b,
        )

    def solved_copy(m, b, slot):
        return neighbour_copy(
            solved_own.at[m], solved_in.at[m, slot], solved_send.at[m, b], solved_recv.at[m, slot], b
        )

    def each_face(body, faces=(0, 1, 2, 3)):
        for b in faces:
            @pl.when(has[b])
            def _():
                body(b)

    def pick_rows(index, src, dst):
        def body(step, carry):
            base = step * 32
            for j in range(32):
                dst[pl.ds(base + j, 1), :] = src[pl.ds(index[0, base + j], 1), :]
            return carry

        lax.fori_loop(0, ni // 32, body, 0)

    def to_faces(src, dst):
        pick_rows(pos_smem, src, dst)

    def from_faces(src, dst):
        pick_rows(place_smem, src, dst)

    def over_chunks(body, init=0):
        per_face = face // CHUNK

        def step(i, carry):
            b = i // per_face
            at_in = pl.multiple_of((i - b * per_face) * CHUNK, CHUNK)
            return body(pl.ds(pl.multiple_of(i * CHUNK, CHUNK), CHUNK), b, pl.ds(at_in, CHUNK), carry)

        return lax.fori_loop(0, ni // CHUNK, step, init)

    def apply(matrix, vector, out, out_type):
        rows = ROWS if ni % ROWS == 0 else ni

        def body(i, carry):
            at = pl.ds(pl.multiple_of(i * rows, rows), rows)
            out[at, :] = dot(matrix[at, :], vector[...]).astype(out_type)
            return carry

        lax.fori_loop(0, ni // rows, body, 0)

    for b in range(4):
        @pl.when(jnp.logical_not(has[b]))
        def _():
            def zero_faces(e, carry):
                face_in[e, b] = jnp.zeros((face, nrhs), F32)
                return carry

            def zero_parts(m, carry):
                parts_in[m, b] = jnp.zeros((ncon, nrhs), F32)
                solved_in[m, b] = jnp.zeros((ncon, nrhs), F32)
                return carry

            lax.fori_loop(0, face_in.shape[0], zero_faces, 0)
            lax.fori_loop(0, ITERS + 1, zero_parts, 0)
            basis_in[b] = jnp.zeros((ncon, face), F32)
            tb_in[b] = jnp.zeros(tb_own.shape, F32)
            if b >= 2:
                tinv_in[b - 2] = jnp.zeros(tinv_own.shape, F32)

    spots = (
        lax.broadcasted_iota(jnp.int32, place_vec.shape, 0) * 128
        + lax.broadcasted_iota(jnp.int32, place_vec.shape, 1)
    )

    def invert(step, found):
        for j in range(32):
            k = step * 32 + j
            found = jnp.where(spots == pos_smem[0, k], k, found)
        return found

    place_vec[...] = lax.fori_loop(0, ni // 32, invert, jnp.zeros(place_vec.shape, jnp.int32))
    place_copies = [
        pltpu.make_async_copy(
            place_vec.at[pl.ds(i, 1)], place_smem.at[:, pl.ds(i * 128, 128)], load_sem.at[4 + i]
        )
        for i in range(ni // 128)
    ]
    for copy in place_copies:
        copy.start()

    select = jnp.where(
        lax.broadcasted_iota(jnp.int32, (ncon, ncon), 0) == cmap_row[...], 1.0, 0.0
    ).astype(BF16)
    fetch_basis.wait()
    fetch_loads.wait()
    fetch_inv.start()
    fetch_stiff.start()
    tb_own[...] = jnp.zeros_like(tb_own)
    tb_own[:, 0:topc] = tbasis_ref[...]
    tinv_own[...] = tinv_ref[...]

    def turn_basis(j, carry):
        at = pl.ds(pl.multiple_of(j * 128, 128), 128)
        block = dot(select, basis[:, at])
        prod[at, :] = jnp.concatenate([block, jnp.zeros((128 - ncon, 128), F32)], axis=0).T
        return carry

    lax.fori_loop(0, ni // 128, turn_basis, 0)
    to_faces(prod, local_part)

    def turn_back(j, carry):
        at = pl.ds(pl.multiple_of(j * 128, 128), 128)
        basis_f32[:, at] = local_part[at, :].T[0:ncon]
        return carry

    lax.fori_loop(0, ni // 128, turn_back, 0)
    pl.semaphore_wait(barrier, n_dev - 1 + n_group - 1)
    each_face(lambda b: basis_copy(b, opposite[b]).start())
    each_face(lambda b: tb_copy(b, opposite[b]).start())
    to_faces(loads, field)
    each_face(lambda b: face_copy(field, 0, b, opposite[b]).start())
    each_face(lambda b: tinv_copy(b, opposite[b]).start(), (2, 3))

    def build(i, carry):
        rows = lax.broadcasted_iota(jnp.int32, (64, ni), 0) + i * 64
        at = pl.ds(pl.multiple_of(i * 64, 64), 64)
        perm_t[at, :] = jnp.where(rows == pos_row[...], 1.0, 0.0).astype(BF16)
        return carry

    lax.fori_loop(0, ni // 64, build, 0)

    def clear(at, b, at_in, carry):
        zero = jnp.zeros((CHUNK, nrhs), F32)
        res[at, :] = zero
        dirn[at, :] = zero
        sol[at, :] = zero
        return carry

    over_chunks(clear)
    group_now[...] = jnp.zeros_like(group_now)
    top_now[...] = jnp.zeros_like(top_now)
    step_now[...] = jnp.full(step_now.shape, -1.0, F32)
    norm_now[...] = jnp.ones_like(norm_now)
    ginv_hi[...], ginv_lo[...] = split(ginv_ref[...])

    tb_all[...] = jnp.zeros_like(tb_all)
    each_face(lambda b: tb_copy(b, b).wait_recv())
    tb_all[0:ncon, 0:128] = tb_own[...]
    tb_all[ncon:2 * ncon, 0:128] = tb_in[0]
    tb_all[2 * ncon:3 * ncon, 0:128] = tb_in[1]
    tb_all[3 * ncon:4 * ncon, 128:256] = tb_in[2]
    tb_all[4 * ncon:5 * ncon, 128:256] = pltpu.roll(tb_in[3], 64, 1)
    tb_all[5 * ncon:5 * ncon + 8, 0:128] = jnp.where(
        (lax.broadcasted_iota(jnp.int32, (8, 128), 0) == 0)
        & (lax.broadcasted_iota(jnp.int32, (8, 128), 1) == 64), 1.0, 0.0,
    ).astype(F32)
    tb_all_hi[...], tb_all_lo[...] = split(tb_all[...])
    for copy in place_copies:
        copy.wait()

    basis_all[...] = jnp.zeros_like(basis_all)
    basis_all[0:ncon, :] = basis_f32[...].astype(BF16)
    each_face(lambda b: basis_copy(b, b).wait_recv())
    for b in range(4):
        basis_all[(b + 1) * ncon:(b + 2) * ncon, b * face:(b + 1) * face] = basis_in[b].astype(BF16)

    def set_up_top():
        tinv_all[...] = jnp.zeros_like(tinv_all)
        cols = n_group * topc
        tinv_all[0:topc, 0:cols] = tinv_own[...]
        each_face(lambda b: tinv_copy(b, b).wait_recv(), (2, 3))
        tinv_all[128:128 + topc, 0:cols] = tinv_in[0]
        tinv_all[192:192 + topc, 0:cols] = tinv_in[1]

        def turn_over(j, carry):
            at = pl.ds(pl.multiple_of(j * 128, 128), 128)
            turned[at, :] = tinv_all[:, at].T
            return carry

        lax.fori_loop(0, turned.shape[0] // 128, turn_over, 0)
        t2_hi[...] = jnp.zeros_like(t2_hi)
        t2_lo[...] = jnp.zeros_like(t2_lo)

        def place(q, carry):
            hi, lo = split(turned[pl.ds(pl.multiple_of(q * topc, 16), topc), :])
            at = pl.ds(pl.multiple_of(q * 64, 64), topc)
            t2_hi[at, :] = hi
            t2_lo[at, :] = lo
            return carry

        lax.fori_loop(0, n_group, place, 0)

    def combine():
        for b in range(4):
            at = slice(b * face, (b + 1) * face)
            comb_t[0:ncon, at] = basis_f32[:, at]
            comb_t[ncon:2 * ncon, at] = basis_in[b]
            comb_t[2 * ncon:3 * ncon, at] = basis_f32[:, at]
            comb_t[3 * ncon:4 * ncon, at] = basis_in[b]
        comb_t[4 * ncon:, :] = jnp.zeros((256 - 4 * ncon, ni), F32)

        def turn_over(j, carry):
            at = pl.ds(pl.multiple_of(j * 128, 128), 128)
            comb[at, :] = comb_t[:, at].T.astype(BF16)
            return carry

        lax.fori_loop(0, ni // 128, turn_over, 0)

    odd = lax.rem(g, 2) == 1
    n_pairs = n_group // 2

    def total(buf, k):
        return jnp.sum(jnp.sum(buf[k], axis=0), axis=0, keepdims=True)

    def inner_of_plain():
        return over_chunks(
            lambda at, b, at_in, c: c + fold(plain[at, :].astype(F32) * prod[at, :]), jnp.zeros((8, nrhs), F32)
        )

    def iteration(it, carry):
        later = it > 0

        @pl.when(later)
        def _():
            apply(perm_t, scaled, plain, BF16)

            @pl.when(it == 1)
            def _():
                fetch_stiff.wait()

            apply(stiff, plain, prod, F32)
            curv_dev[it, d] = inner_of_plain()
            spread(lambda p: curv_dev.at[it, d], curv_dev, it, cd_send, cd_recv, True)
            to_faces(prod, field)

        def halves(at, b, at_in, c):
            hi, lo = split(weight_of(b) * field[at, :])
            scaled[at, :] = hi
            scaled_lo[at, :] = lo
            return c

        over_chunks(halves)
        shares = dot(basis_all[...], scaled[...]) + dot(basis_all[...], scaled_lo[...])
        parts[it] = shares
        u_t = dot3(split(shares.T), (tb_all_hi[...], tb_all_lo[...]))
        u_out[it, :, 0] = u_t[:, 0:128].reshape(n_dev, per_dev, 128)
        u_out[it, :, 1] = u_t[:, 128:256].reshape(n_dev, per_dev, 128)
        u_in[it, d] = u_out[it, d]
        spread(lambda p: u_out.at[it, p], u_in, it, u_send, u_recv, True)
        each_face(lambda b: parts_copy(it, b, opposite[b]).start())

        @pl.when(later)
        def _():
            each_face(lambda b: face_copy(field, 2 * it, b, opposite[b]).start())

        @pl.when(it == 0)
        def _():
            set_up_top()

        each_face(lambda b: parts_copy(it, b, b).wait_recv())
        own_coarse = parts[it, 0:ncon] + (
            (parts_in[it, 0] + parts_in[it, 1]) + (parts_in[it, 2] + parts_in[it, 3])
        )
        coarse[it, d] = own_coarse
        spread(lambda p: coarse.at[it, d], coarse, it, coarse_send, coarse_recv, True)

        @pl.when(later)
        def _():
            all_of(curv_dev, it, cd_send, cd_recv, True).wait_recv()
            curv_group[it, g] = jnp.sum(curv_dev[it], axis=0)
            spread(lambda p: curv_group.at[it, g], curv_group, it, cg_send, cg_recv, False)

        all_of(u_in, it, u_send, u_recv, True).wait_recv()
        own_tile = jnp.sum(u_in[it, :, 0], axis=0)
        side_tile = jnp.sum(u_in[it, :, 1], axis=0)
        lane = lax.broadcasted_iota(jnp.int32, own_tile.shape, 1)
        keep = jnp.where(odd, lane, 127 - lane) < 64
        top_in[it, g, 0] = jnp.where(odd, pltpu.roll(own_tile, 64, 1), own_tile) + jnp.where(
            keep, side_tile, 0.0
        )
        top_in[it, g, 1] = pltpu.roll(jnp.where(keep, 0.0, side_tile), 64, 1)
        spread(lambda p: top_in.at[it, g], top_in, it, top_send, top_recv, False)

        @pl.when(it == 0)
        def _():
            combine()

        @pl.when(later)
        def _():
            @pl.when(it == 1)
            def _():
                all_of(dot_group, 0, dg_send, dg_recv, False).wait_recv()
                norm_now[...] = total(dot_group, 0)

            all_of(curv_group, it, cg_send, cg_recv, False).wait_recv()
            step_now[...] = norm_now[...] / total(curv_group, it)

        step_size = step_now[...]
        step_cols[...] = jnp.broadcast_to(step_size, step_cols.shape).T
        step_col = step_cols[pl.ds(pl.multiple_of(d * per_dev, per_dev), per_dev), :]

        all_of(top_in, it, top_send, top_recv, False).wait_recv()
        every = top_in[it]
        pairs = []
        for p in range(n_pairs):
            pair = every[2 * p, 0] + every[2 * p + 1, 0]
            if p > 0:
                pair = pair + every[2 * p - 1, 1]
            if p < n_pairs - 1:
                pair = pair + every[2 * p + 2, 1]
            pairs.append(top_now[:, p * 128:(p + 1) * 128] - step_col * pair)
        top_next = jnp.concatenate(pairs, axis=1)
        top_now[...] = top_next
        ts = dot3(split(top_next), (t2_hi[...], t2_lo[...]))
        own_pair = top_now[:, pl.ds(pl.multiple_of(g // 2 * 128, 128), 128)]
        own_top = jnp.where(odd, pltpu.roll(own_pair, 64, 1), own_pair)
        top_energy = jnp.sum(jnp.where(lane < topc, ts[:, 0:128] * own_top, 0.0), axis=1, keepdims=True)
        ts_in[it, d, 0] = jnp.where(lane == 64, top_energy, ts[:, 0:128])
        ts_in[it, d, 1] = ts[:, 128:256]
        spread(lambda p: ts_in.at[it, d], ts_in, it, ts_send, ts_recv, True)

        each_face(lambda b: face_copy(field, 2 * it, b, b).wait_recv())

        def update(at, b, at_in, c):
            value = res[at, :] - step_size * (field[at, :] + face_in[2 * it, b, at_in, :])
            res[at, :] = value
            scaled[at, :] = (weight_of(b) * value).astype(BF16)
            return c

        over_chunks(update)

        apply(perm_t, scaled, plain, BF16)

        @pl.when(it == 0)
        def _():
            fetch_inv.wait()

        apply(inv, plain, prod, F32)

        all_of(coarse, it, coarse_send, coarse_recv, True).wait_recv()
        group_next = group_now[...] - step_size * coarse[it].reshape(n_dev * ncon, nrhs)
        group_now[...] = group_next
        solved = dot3((ginv_hi[...], ginv_lo[...]), split(group_next))
        solved_own[it] = solved
        each_face(lambda b: solved_copy(it, b, opposite[b]).start())

        energy = inner_of_plain()
        own_coarse_now = group_now[pl.ds(pl.multiple_of(d * ncon, 16), ncon), :]
        dot_dev[it, d] = energy + fold(own_coarse_now * solved)
        spread(lambda p: dot_dev.at[it, d], dot_dev, it, dd_send, dd_recv, True)
        to_faces(prod, local_part)
        each_face(lambda b: face_copy(local_part, 2 * it + 1, b, opposite[b]).start())

        def advance(at, b, at_in, c):
            sol[at, :] = sol[at, :] + step_size * dirn[at, :]
            return c

        over_chunks(advance)

        @pl.when(it == ITERS)
        def _():
            from_faces(sol, loads)
            pltpu.make_async_copy(loads, x_out, out_sem.at[0]).start()
            from_faces(res, weighted)
            pltpu.make_async_copy(weighted, r_out, out_sem.at[1]).start()

        all_of(ts_in, it, ts_send, ts_recv, True).wait_recv()
        ts_all = jnp.concatenate(
            [ts_in[it, :, 0].reshape(nrhs, 128), ts_in[it, :, 1].reshape(nrhs, 128)], axis=1
        )
        upper[...] = dot3((tb_all_hi[...], tb_all_lo[...]), split(ts_all), NT)

        all_of(dot_dev, it, dd_send, dd_recv, True).wait_recv()
        line = lax.broadcasted_iota(jnp.int32, (8, nrhs), 0)
        dot_group[it, g] = jnp.sum(dot_dev[it], axis=0) + jnp.where(
            line == 0, upper[5 * ncon:5 * ncon + 1, :], 0.0
        )
        spread(lambda p: dot_group.at[it, g], dot_group, it, dg_send, dg_recv, False)

        own_hi, own_lo = split(solved + upper[0:ncon, :])
        each_face(lambda b: solved_copy(it, b, b).wait_recv())
        each_face(lambda b: face_copy(local_part, 2 * it + 1, b, b).wait_recv())

        def join(b, c):
            above = upper[pl.ds(pl.multiple_of((b + 1) * ncon, 16), ncon), :]
            in_hi, in_lo = split(solved_in[it, b] + above)
            values = jnp.concatenate(
                [own_hi, in_hi, own_lo, in_lo, jnp.zeros((256 - 4 * ncon, nrhs), BF16)], axis=0
            )
            at = pl.ds(pl.multiple_of(b * face, face), face)
            prod[at, :] = weight_of(b) * (
                local_part[at, :] + face_in[2 * it + 1, b] + dot(comb[at, :], values)
            )
            return c

        lax.fori_loop(0, 4, join, 0)

        all_of(u_in, it, u_send, u_recv, True).wait_send()
        all_of(coarse, it, coarse_send, coarse_recv, True).wait_send()
        all_of(top_in, it, top_send, top_recv, False).wait_send()
        all_of(ts_in, it, ts_send, ts_recv, True).wait_send()
        all_of(dot_dev, it, dd_send, dd_recv, True).wait_send()

        def left(b):
            face_copy(field, 2 * it, b, opposite[b]).wait_send()
            face_copy(local_part, 2 * it + 1, b, opposite[b]).wait_send()
            parts_copy(it, b, opposite[b]).wait_send()
            solved_copy(it, b, opposite[b]).wait_send()

        each_face(left)

        @pl.when(later)
        def _():
            all_of(curv_dev, it, cd_send, cd_recv, True).wait_send()
            all_of(curv_group, it, cg_send, cg_recv, False).wait_send()
            all_of(dot_group, it, dg_send, dg_recv, False).wait_recv()
            norm_next = total(dot_group, it)
            step_now[...] = norm_next / norm_now[...]
            norm_now[...] = norm_next

        ratio = step_now[...]

        def turn(at, b, at_in, c):
            value = prod[at, :] + ratio * dirn[at, :]
            dirn[at, :] = value
            scaled[at, :] = value.astype(BF16)
            return c

        over_chunks(turn)
        return carry

    lax.fori_loop(0, ITERS + 1, iteration, 0)

    from_faces(dirn, prod)
    store = pltpu.make_async_copy(prod, d_out, out_sem.at[2])
    store.start()
    for m in range(ITERS + 1):
        all_of(dot_group, m, dg_send, dg_recv, False).wait_send()
    each_face(lambda b: basis_copy(b, opposite[b]).wait_send())
    each_face(lambda b: tb_copy(b, opposite[b]).wait_send())
    each_face(lambda b: tinv_copy(b, opposite[b]).wait_send(), (2, 3))
    pltpu.make_async_copy(loads, x_out, out_sem.at[0]).wait()
    pltpu.make_async_copy(weighted, r_out, out_sem.at[1]).wait()
    store.wait()


def local(
    n_group, n_dev,
    applied_loads, stiffness, local_inverse, coarse_basis, face_index, coarse_map, group_inverse, top_basis, top_inverse,
):
    ni, nrhs = applied_loads.shape[1:]
    ncon = coarse_basis.shape[1]
    topc = top_basis.shape[1]
    face = ni // 4
    per_dev = nrhs // n_dev
    uses = ITERS + 1
    exchanges = 2 * uses
    top_rows = n_group * 64
    top_pad = (n_group * topc + 127) // 128 * 128
    vmem = pl.BlockSpec(memory_space=pltpu.VMEM)
    smem = pl.BlockSpec(memory_space=pltpu.SMEM)
    hbm = pl.BlockSpec(memory_space=pl.ANY)
    field = jax.ShapeDtypeStruct((ni, nrhs), F32)
    dma = pltpu.SemaphoreType.DMA

    def f32(*shape):
        return pltpu.VMEM(shape, F32)

    def bf16(*shape):
        return pltpu.VMEM(shape, BF16)

    scratch = [
        f32(ni, nrhs), bf16(ni, ni), bf16(ni, ni), bf16(ncon, ni), bf16(ni, ni),
        pltpu.VMEM((ni // 128, 128), jnp.int32), pltpu.SMEM((1, ni), jnp.int32),
        f32(ni, nrhs),
        f32(ni, nrhs), f32(ni, nrhs), f32(ni, nrhs), f32(ni, nrhs), f32(ni, nrhs), f32(ni, nrhs),
        bf16(ni, nrhs), bf16(ni, nrhs), bf16(ni, nrhs),
        f32(exchanges, 4, face, nrhs), f32(ncon, ni), f32(4, ncon, face), bf16(256, ni), f32(256, ni), bf16(ni, 256),
        bf16(ncon, n_dev * ncon), bf16(ncon, n_dev * ncon),
        f32(256, 256), bf16(256, 256), bf16(256, 256),
        bf16(top_rows, 256), bf16(top_rows, 256), f32(256, top_pad), f32(top_pad, 256),
        f32(ncon, 128), f32(4, ncon, 128), f32(topc, n_group * topc), f32(2, topc, n_group * topc), f32(256, nrhs),
        f32(uses, 256, nrhs), f32(uses, 4, ncon, nrhs), f32(uses, n_dev, ncon, nrhs),
        f32(uses, n_dev, 2, per_dev, 128), f32(uses, n_dev, 2, per_dev, 128),
        f32(uses, n_group, 2, per_dev, 128), f32(uses, n_dev, 2, per_dev, 128),
        f32(uses, ncon, nrhs), f32(uses, 4, ncon, nrhs),
        f32(n_dev * ncon, nrhs), f32(per_dev, n_group * 64), f32(1, nrhs), f32(nrhs, nrhs), f32(1, nrhs),
        f32(uses, n_dev, 8, nrhs), f32(uses, n_group, 8, nrhs),
        f32(uses, n_dev, 8, nrhs), f32(uses, n_group, 8, nrhs),
        dma((4 + ni // 128,)), dma((3,)), dma((exchanges, 4)), dma((exchanges, 4)),
        dma((4,)), dma((4,)), dma((4,)), dma((4,)), dma((2,)), dma((2,)),
        dma((uses, 4)), dma((uses, 4)), dma((uses, 4)), dma((uses, 4)),
    ] + [dma((uses,))] * 16
    x, r, dirn, one = pl.pallas_call(
        functools.partial(main_kernel, n_group, n_dev),
        out_shape=[field] * 3 + [jax.ShapeDtypeStruct((1, nrhs), F32)],
        in_specs=[hbm, hbm, hbm, hbm, smem, vmem, vmem, vmem, vmem, vmem],
        out_specs=[hbm] * 3 + [vmem],
        scratch_shapes=scratch,
        compiler_params=pltpu.CompilerParams(
            collective_id=0, has_side_effects=True, vmem_limit_bytes=56 * 2**20
        ),
        cost_estimate=pl.CostEstimate(
            flops=18 * ni * ni * nrhs, bytes_accessed=4 * ni * ni + 24 * ni * nrhs, transcendentals=0
        ),
        name="pcg",
    )(
        applied_loads[0], stiffness[0], local_inverse[0], coarse_basis[0],
        face_index, face_index, coarse_map, group_inverse, top_basis, top_inverse,
    )
    return (x * one)[None], (r * one)[None], (dirn * one)[None]


def solution(mesh):
    both = ("group", "dev")
    return jax.shard_map(
        functools.partial(local, mesh.shape["group"], mesh.shape["dev"]),
        mesh=mesh,
        in_specs=(
            P(both, None, None), P(both, None, None), P(both, None, None), P(both, None, None),
            P(both, None), P(both, None), P(both, None), P(both, None), P("group", None),
        ),
        out_specs=(P(both, None, None),) * 3,
        check_vma=False,
    )
```

time: 868 us -> 124 us (0.14); the launches traced: 859 us -> 124 us
  blocking collectives: 641 us -> 0 us
  Pallas kernels: 0 us -> 121 us
  other arithmetic: 66.4 us -> 3.06 us
  starting transfers between devices: 54 us -> 0 us
  waiting for transfers between devices: 33.1 us -> 0 us
  matrix products: 32 us -> 0 us
  local copies, waits for them, and re-layouts: 30.2 us -> 0 us
    psum x7 -> x0, blocking collectives: 471 us -> none  [the longest x4 297 us: global_sum(): lax.psum(jnp.sum(factor * left_side * right_side, axis=0), ('group', 'dev'))]
    all_gather x6 -> x0, blocking collectives: 170 us -> none  [the longest x3 113 us: precondition(): stacked = lax.all_gather(reduced, 'group', axis=0, tiled=True)]
    pallas_call x0 -> x1, Pallas kernels: none -> 121 us  [local(): pl.pallas_call(functools.partial(main_kernel, n_group, n_dev), out_shape=...]
    scatter-add x6 -> x0, other arithmetic: 55.8 us -> none  [assemble(): return field.at[positions].add(partner.reshape(dof_count, rhs_count))]
    ppermute x24 -> x0, starting transfers between devices: 54 us -> none  [the longest x12 32.3 us: with_halo(): lax.ppermute(lax.slice_in_dim(block, block.shape[dim] - width, None, axis...]
    ppermute x24 -> x0, waiting for transfers between devices: 33.1 us -> none  [the longest x12 27.2 us: with_halo(): lax.ppermute(lax.slice_in_dim(block, 0, width, axis=dim), axis, backward)]
    dot_general x29 -> x0, matrix products: 32 us -> none  [the longest x3 13 us: precondition(): jnp.dot(inverse_block, scaled_res, preferred_element_type=jnp.float32)]
    gather x6 -> x0, local copies, waits for them, and re-layouts: 18.9 us -> none  [assemble(): jnp.take(field, positions, axis=0).reshape(4, face_width, rhs_count)]
  transfers between devices with their start and end apart: 24 -> 0, of which waited for: 16 -> 0; matrix products, arithmetic and copies ran while one was open for 1% -> 0% of each run, Pallas kernels for 0% -> 0%
where the time goes in v2:
time: 124 us
  Pallas kernels  121 us (98%)
  other arithmetic  3.06 us (2%)
    pallas_call x1, Pallas kernels, local(): pl.pallas_call(functools.partial(main_kernel, n_group, n_dev), out_shape=...  121 us
    broadcast_in_dim x1, other arithmetic, local(): return ((x * one)[None], (r * one)[None], (dirn * one)[None])  3.06 us

profile of v2, /device:TPU:1, one launch (start us, length us, event | category | flops | bytes accessed | tf_op | source)
XLA Modules:
  0.0 124.3 jit_solution(9894558321813103469)
XLA Ops:
  0.6 120.6 %pcg.1 = (f32[1536,128]{1,0:T(8,128)}, f32[1536,128]{1,0:T(8,128)}, f32[1536,128]{1,0:T(8,128)}, f32[1,128]{1,0:T(1,128)}) custom-call(f32[1536,128]{1,0:T(8,128)} %bitcast.14, bf16[1536,1536]{1,0:T(8,128)(2,1)} %bitcast.12, bf16[1536,1536]{1,0:T(8,128)(2,1)} %bitcast.13, bf16[48,1536]{1,0:T(8,128)(2,1)} %bitcast.15, s32[1,1536]{1,0:T(1,128)} %pos_row.1, ...), custom_call_target="tpu_custom_call" | custom-call | flops 5435817984 | bytes 14155776 | tf_op jit(solution)/shard_map/pcg/pallas_call | solution.py:643
  121.2 3.1 %multiply_bitcast_fusion = (f32[1,1536,128]{2,1,0:T(8,128)}, f32[1,1536,128]{2,1,0:T(8,128)}, f32[1,1536,128]{2,1,0:T(8,128)}) fusion(f32[1536,128]{1,0:T(8,128)} %get-tuple-element.10, f32[128]{0:T(128)} %bitcast.11, f32[1536,128]{1,0:T(8,128)} %get-tuple-element.9, f32[1536,128]{1,0:T(8,128)} %get-tuple-element.7), kind=kLoop, calls=%fused_computation | loop fusion | flops 589824 | bytes 4719104 | tf_op jit(solution)/shard_map/broadcast_in_dim | solution.py:660

commit v3 on v2

--- a/solution.py
+++ b/solution.py
@@ -14,7 +14,7 @@
 NN = (((1,), (0,)), ((), ()))
 NT = (((1,), (1,)), ((), ()))
 CHUNK = 128
-ROWS = 512
+ROWS = 768
 
 
 def dot(a, b, dims=NN):
@@ -38,10 +38,10 @@
 
 def main_kernel(
     n_group, n_dev,
-    loads_hbm, stiff_hbm, inv_hbm, basis_hbm, pos_smem, pos_row, cmap_row, ginv_ref, tbasis_ref, tinv_ref,
+    loads_hbm, stiff_hbm, inv_hbm, basis_hbm, pos_smem, cmap_row, ginv_ref, tbasis_ref, tinv_ref,
     x_out, r_out, d_out, one_out,
-    loads, stiff, inv, basis, perm_t, place_vec, place_smem,
-    field, local_part, res, dirn, sol, prod, weighted, scaled, scaled_lo, plain,
+    loads, stiff, inv, basis, place_vec, place_smem,
+    field, local_part, res, dirn, sol, prod, joined, weight, scaled, scaled_lo, plain,
     face_in, basis_f32, basis_in, basis_all, comb_t, comb,
     ginv_hi, ginv_lo, tb_all, tb_all_hi, tb_all_lo, t2_hi, t2_lo, tinv_all, turned,
     tb_own, tb_in, tinv_own, tinv_in, upper,
@@ -164,12 +164,12 @@
 
     def pick_rows(index, src, dst):
         def body(step, carry):
-            base = step * 32
-            for j in range(32):
+            base = step * 64
+            for j in range(64):
                 dst[pl.ds(base + j, 1), :] = src[pl.ds(index[0, base + j], 1), :]
             return carry
 
-        lax.fori_loop(0, ni // 32, body, 0)
+        lax.fori_loop(0, ni // 64, body, 0)
 
     def to_faces(src, dst):
         pick_rows(pos_smem, src, dst)
@@ -222,12 +222,12 @@
     )
 
     def invert(step, found):
-        for j in range(32):
-            k = step * 32 + j
+        for j in range(64):
+            k = step * 64 + j
             found = jnp.where(spots == pos_smem[0, k], k, found)
         return found
 
-    place_vec[...] = lax.fori_loop(0, ni // 32, invert, jnp.zeros(place_vec.shape, jnp.int32))
+    place_vec[...] = lax.fori_loop(0, ni // 64, invert, jnp.zeros(place_vec.shape, jnp.int32))
     place_copies = [
         pltpu.make_async_copy(
             place_vec.at[pl.ds(i, 1)], place_smem.at[:, pl.ds(i * 128, 128)], load_sem.at[4 + i]
@@ -270,19 +270,12 @@
     each_face(lambda b: face_copy(field, 0, b, opposite[b]).start())
     each_face(lambda b: tinv_copy(b, opposite[b]).start(), (2, 3))
 
-    def build(i, carry):
-        rows = lax.broadcasted_iota(jnp.int32, (64, ni), 0) + i * 64
-        at = pl.ds(pl.multiple_of(i * 64, 64), 64)
-        perm_t[at, :] = jnp.where(rows == pos_row[...], 1.0, 0.0).astype(BF16)
-        return carry
-
-    lax.fori_loop(0, ni // 64, build, 0)
-
     def clear(at, b, at_in, carry):
         zero = jnp.zeros((CHUNK, nrhs), F32)
         res[at, :] = zero
         dirn[at, :] = zero
         sol[at, :] = zero
+        joined[at, :] = jnp.zeros((CHUNK, nrhs), F32) + weight_of(b)
         return carry
 
     over_chunks(clear)
@@ -306,6 +299,7 @@
     tb_all_hi[...], tb_all_lo[...] = split(tb_all[...])
     for copy in place_copies:
         copy.wait()
+    from_faces(joined, weight)
 
     basis_all[...] = jnp.zeros_like(basis_all)
     basis_all[0:ncon, :] = basis_f32[...].astype(BF16)
@@ -371,8 +365,6 @@
 
         @pl.when(later)
         def _():
-            apply(perm_t, scaled, plain, BF16)
-
             @pl.when(it == 1)
             def _():
                 fetch_stiff.wait()
@@ -434,6 +426,15 @@
         def _():
             combine()
 
+        each_face(lambda b: face_copy(field, 2 * it, b, b).wait_recv())
+
+        def assemble(at, b, at_in, c):
+            joined[at, :] = field[at, :] + face_in[2 * it, b, at_in, :]
+            return c
+
+        over_chunks(assemble)
+        from_faces(joined, prod)
+
         @pl.when(later)
         def _():
             @pl.when(it == 1)
@@ -447,6 +448,20 @@
         step_size = step_now[...]
         step_cols[...] = jnp.broadcast_to(step_size, step_cols.shape).T
         step_col = step_cols[pl.ds(pl.multiple_of(d * per_dev, per_dev), per_dev), :]
+
+        def update(at, b, at_in, c):
+            value = res[at, :] - step_size * prod[at, :]
+            res[at, :] = value
+            plain[at, :] = (weight[at, :] * value).astype(BF16)
+            return c
+
+        over_chunks(update)
+
+        @pl.when(it == 0)
+        def _():
+            fetch_inv.wait()
+
+        apply(inv, plain, prod, F32)
 
         all_of(top_in, it, top_send, top_recv, False).wait_recv()
         every = top_in[it]
@@ -468,24 +483,6 @@
         ts_in[it, d, 1] = ts[:, 128:256]
         spread(lambda p: ts_in.at[it, d], ts_in, it, ts_send, ts_recv, True)
 
-        each_face(lambda b: face_copy(field, 2 * it, b, b).wait_recv())
-
-        def update(at, b, at_in, c):
-            value = res[at, :] - step_size * (field[at, :] + face_in[2 * it, b, at_in, :])
-            res[at, :] = value
-            scaled[at, :] = (weight_of(b) * value).astype(BF16)
-            return c
-
-        over_chunks(update)
-
-        apply(perm_t, scaled, plain, BF16)
-
-        @pl.when(it == 0)
-        def _():
-            fetch_inv.wait()
-
-        apply(inv, plain, prod, F32)
-
         all_of(coarse, it, coarse_send, coarse_recv, True).wait_recv()
         group_next = group_now[...] - step_size * coarse[it].reshape(n_dev * ncon, nrhs)
         group_now[...] = group_next
@@ -508,10 +505,8 @@
 
         @pl.when(it == ITERS)
         def _():
-            from_faces(sol, loads)
-            pltpu.make_async_copy(loads, x_out, out_sem.at[0]).start()
-            from_faces(res, weighted)
-            pltpu.make_async_copy(weighted, r_out, out_sem.at[1]).start()
+            pltpu.make_async_copy(sol, x_out, out_sem.at[0]).start()
+            pltpu.make_async_copy(res, r_out, out_sem.at[1]).start()
 
         all_of(ts_in, it, ts_send, ts_recv, True).wait_recv()
         ts_all = jnp.concatenate(
@@ -537,12 +532,13 @@
                 [own_hi, in_hi, own_lo, in_lo, jnp.zeros((256 - 4 * ncon, nrhs), BF16)], axis=0
             )
             at = pl.ds(pl.multiple_of(b * face, face), face)
-            prod[at, :] = weight_of(b) * (
+            joined[at, :] = weight_of(b) * (
                 local_part[at, :] + face_in[2 * it + 1, b] + dot(comb[at, :], values)
             )
             return c
 
         lax.fori_loop(0, 4, join, 0)
+        from_faces(joined, prod)
 
         all_of(u_in, it, u_send, u_recv, True).wait_send()
         all_of(coarse, it, coarse_send, coarse_recv, True).wait_send()
@@ -572,7 +568,7 @@
         def turn(at, b, at_in, c):
             value = prod[at, :] + ratio * dirn[at, :]
             dirn[at, :] = value
-            scaled[at, :] = value.astype(BF16)
+            plain[at, :] = value.astype(BF16)
             return c
 
         over_chunks(turn)
@@ -580,16 +576,15 @@
 
     lax.fori_loop(0, ITERS + 1, iteration, 0)
 
-    from_faces(dirn, prod)
-    store = pltpu.make_async_copy(prod, d_out, out_sem.at[2])
+    store = pltpu.make_async_copy(dirn, d_out, out_sem.at[2])
     store.start()
     for m in range(ITERS + 1):
         all_of(dot_group, m, dg_send, dg_recv, False).wait_send()
     each_face(lambda b: basis_copy(b, opposite[b]).wait_send())
     each_face(lambda b: tb_copy(b, opposite[b]).wait_send())
     each_face(lambda b: tinv_copy(b, opposite[b]).wait_send(), (2, 3))
-    pltpu.make_async_copy(loads, x_out, out_sem.at[0]).wait()
-    pltpu.make_async_copy(weighted, r_out, out_sem.at[1]).wait()
+    pltpu.make_async_copy(sol, x_out, out_sem.at[0]).wait()
+    pltpu.make_async_copy(res, r_out, out_sem.at[1]).wait()
     store.wait()
 
 
@@ -619,10 +614,10 @@
         return pltpu.VMEM(shape, BF16)
 
     scratch = [
-        f32(ni, nrhs), bf16(ni, ni), bf16(ni, ni), bf16(ncon, ni), bf16(ni, ni),
+        f32(ni, nrhs), bf16(ni, ni), bf16(ni, ni), bf16(ncon, ni),
         pltpu.VMEM((ni // 128, 128), jnp.int32), pltpu.SMEM((1, ni), jnp.int32),
         f32(ni, nrhs),
-        f32(ni, nrhs), f32(ni, nrhs), f32(ni, nrhs), f32(ni, nrhs), f32(ni, nrhs), f32(ni, nrhs),
+        f32(ni, nrhs), f32(ni, nrhs), f32(ni, nrhs), f32(ni, nrhs), f32(ni, nrhs), f32(ni, nrhs), f32(ni, nrhs),
         bf16(ni, nrhs), bf16(ni, nrhs), bf16(ni, nrhs),
         f32(exchanges, 4, face, nrhs), f32(ncon, ni), f32(4, ncon, face), bf16(256, ni), f32(256, ni), bf16(ni, 256),
         bf16(ncon, n_dev * ncon), bf16(ncon, n_dev * ncon),
@@ -643,7 +638,7 @@
     x, r, dirn, one = pl.pallas_call(
         functools.partial(main_kernel, n_group, n_dev),
         out_shape=[field] * 3 + [jax.ShapeDtypeStruct((1, nrhs), F32)],
-        in_specs=[hbm, hbm, hbm, hbm, smem, vmem, vmem, vmem, vmem, vmem],
+        in_specs=[hbm, hbm, hbm, hbm, smem, vmem, vmem, vmem, vmem],
         out_specs=[hbm] * 3 + [vmem],
         scratch_shapes=scratch,
         compiler_params=pltpu.CompilerParams(
@@ -655,7 +650,7 @@
         name="pcg",
     )(
         applied_loads[0], stiffness[0], local_inverse[0], coarse_basis[0],
-        face_index, face_index, coarse_map, group_inverse, top_basis, top_inverse,
+        face_index, coarse_map, group_inverse, top_basis, top_inverse,
     )
     return (x * one)[None], (r * one)[None], (dirn * one)[None]
 

time: 124 us -> 114 us (0.919)
  Pallas kernels: 121 us -> 110 us
    pallas_call x1, Pallas kernels: 121 us -> 110 us  [local(): pl.pallas_call(functools.partial(main_kernel, n_group, n_dev), out_shape=...]
where the time goes in v3:
time: 114 us
  Pallas kernels  110 us (96%)
  other arithmetic  3.06 us (3%)
    pallas_call x1, Pallas kernels, local(): pl.pallas_call(functools.partial(main_kernel, n_group, n_dev), out_shape=...  110 us
    broadcast_in_dim x1, other arithmetic, local(): return ((x * one)[None], (r * one)[None], (dirn * one)[None])  3.06 us

profile of v3, /device:TPU:1, one launch (start us, length us, event | category | flops | bytes accessed | tf_op | source)
XLA Modules:
  0.0 114.0 jit_solution(18035202283456823843)
XLA Ops:
  0.6 110.3 %pcg.1 = (f32[1536,128]{1,0:T(8,128)}, f32[1536,128]{1,0:T(8,128)}, f32[1536,128]{1,0:T(8,128)}, f32[1,128]{1,0:T(1,128)}) custom-call(f32[1536,128]{1,0:T(8,128)} %bitcast.14, bf16[1536,1536]{1,0:T(8,128)(2,1)} %bitcast.12, bf16[1536,1536]{1,0:T(8,128)(2,1)} %bitcast.13, bf16[48,1536]{1,0:T(8,128)(2,1)} %bitcast.15, s32[1,1536]{1,0:T(1,128)} %pos_smem.1, ...), custom_call_target="tpu_custom_call" | custom-call | flops 5435817984 | bytes 14155776 | tf_op jit(solution)/shard_map/pcg/pallas_call | solution.py:638
  110.9 3.1 %multiply_bitcast_fusion = (f32[1,1536,128]{2,1,0:T(8,128)}, f32[1,1536,128]{2,1,0:T(8,128)}, f32[1,1536,128]{2,1,0:T(8,128)}) fusion(f32[1536,128]{1,0:T(8,128)} %get-tuple-element.10, f32[128]{0:T(128)} %bitcast.11, f32[1536,128]{1,0:T(8,128)} %get-tuple-element.9, f32[1536,128]{1,0:T(8,128)} %get-tuple-element.7), kind=kLoop, calls=%fused_computation | loop fusion | flops 589824 | bytes 4719104 | tf_op jit(solution)/shard_map/broadcast_in_dim | solution.py:655

commit v4 on v3

--- a/solution.py
+++ b/solution.py
@@ -113,7 +113,7 @@
             ).start()
             return carry
 
-        lax.fori_loop(1, n, body, 0)
+        lax.fori_loop(1, n, body, 0, unroll=5)
 
     def all_of(buf, k, send, recv, along_dev):
         n = n_dev if along_dev else n_group
@@ -164,12 +164,12 @@
 
     def pick_rows(index, src, dst):
         def body(step, carry):
-            base = step * 64
-            for j in range(64):
+            base = step * 128
+            for j in range(128):
                 dst[pl.ds(base + j, 1), :] = src[pl.ds(index[0, base + j], 1), :]
             return carry
 
-        lax.fori_loop(0, ni // 64, body, 0)
+        lax.fori_loop(0, ni // 128, body, 0)
 
     def to_faces(src, dst):
         pick_rows(pos_smem, src, dst)
@@ -222,12 +222,12 @@
     )
 
     def invert(step, found):
-        for j in range(64):
-            k = step * 64 + j
+        for j in range(128):
+            k = step * 128 + j
             found = jnp.where(spots == pos_smem[0, k], k, found)
         return found
 
-    place_vec[...] = lax.fori_loop(0, ni // 64, invert, jnp.zeros(place_vec.shape, jnp.int32))
+    place_vec[...] = lax.fori_loop(0, ni // 128, invert, jnp.zeros(place_vec.shape, jnp.int32))
     place_copies = [
         pltpu.make_async_copy(
             place_vec.at[pl.ds(i, 1)], place_smem.at[:, pl.ds(i * 128, 128)], load_sem.at[4 + i]

time: 114 us -> 113 us (level)
  no operation moved by 1% of the time
where the time goes in v4:
time: 113 us
  Pallas kernels  110 us (97%)
  other arithmetic  3.06 us (3%)
    pallas_call x1, Pallas kernels, local(): pl.pallas_call(functools.partial(main_kernel, n_group, n_dev), out_shape=...  110 us
    broadcast_in_dim x1, other arithmetic, local(): return ((x * one)[None], (r * one)[None], (dirn * one)[None])  3.06 us

profile of v4, /device:TPU:1, one launch (start us, length us, event | category | flops | bytes accessed | tf_op | source)
XLA Modules:
  0.0 113.3 jit_solution(2258543247735163135)
XLA Ops:
  0.6 109.6 %pcg.1 = (f32[1536,128]{1,0:T(8,128)}, f32[1536,128]{1,0:T(8,128)}, f32[1536,128]{1,0:T(8,128)}, f32[1,128]{1,0:T(1,128)}) custom-call(f32[1536,128]{1,0:T(8,128)} %bitcast.14, bf16[1536,1536]{1,0:T(8,128)(2,1)} %bitcast.12, bf16[1536,1536]{1,0:T(8,128)(2,1)} %bitcast.13, bf16[48,1536]{1,0:T(8,128)(2,1)} %bitcast.15, s32[1,1536]{1,0:T(1,128)} %pos_smem.1, ...), custom_call_target="tpu_custom_call" | custom-call | flops 5435817984 | bytes 14155776 | tf_op jit(solution)/shard_map/pcg/pallas_call | solution.py:638
  110.2 3.1 %multiply_bitcast_fusion = (f32[1,1536,128]{2,1,0:T(8,128)}, f32[1,1536,128]{2,1,0:T(8,128)}, f32[1,1536,128]{2,1,0:T(8,128)}) fusion(f32[1536,128]{1,0:T(8,128)} %get-tuple-element.10, f32[128]{0:T(128)} %bitcast.11, f32[1536,128]{1,0:T(8,128)} %get-tuple-element.9, f32[1536,128]{1,0:T(8,128)} %get-tuple-element.7), kind=kLoop, calls=%fused_computation | loop fusion | flops 589824 | bytes 4719104 | tf_op jit(solution)/shard_map/broadcast_in_dim | solution.py:655
